TPU v7x, 32 devices: a whole 2x2x4 slice. The times are simulated.
32 devices in a mesh: clips: 2 (over y), tm: 4 (over z), rows: 4 (over x, core).
Axes of the slice: x: 2, y: 2, z: 4, core: 2. Of those that a mesh axis runs over, the one named last changes fastest.
Arguments:
- latents: bfloat16 [32, 8, 192, 128], P(('clips', 'tm'), 'rows'), parts along dimension 0, may hold values from -6 to 6
- conv_weight: bfloat16 [3, 27, 192, 192], replicated, may hold values from -0.078125 to 0.078125
- norm_gains: float32 [3, 192], replicated, may hold values from 0.5 to 1.5
- biases: float32 [3, 192], replicated, may hold values from -3 to 3
Outputs:
- decoded: bfloat16 [32, 8, 192, 128], P(('clips', 'tm'), 'rows'), parts along dimension 0
There are 2 independent parts, one for each index of `clips`. A program takes and returns all parts, laid end to end along the dimension named above; an argument that names none is the same for every part. Nothing has to cross between parts.
All inputs are finite; a program needn't handle non-finite values.
Results may differ from a plain program's by a relative error of at most 0.011.
Values may be sent and summed in bfloat16 or wider, within the bound.
No kernel may reach another device: no remote copies, remote signals or barrier semaphores. Data moves between devices by JAX's collectives and lax.ppermute only.
A program may use at most 64 MiB of HBM per device.

v0:
```python
import jax
import jax.numpy as jnp
from jax import lax
from jax.sharding import PartitionSpec as P

LAYERS = 3


EPSILON = 1e-06


def passed_along(block, axis, distance):
    devices = range(lax.axis_size(axis))
    route = [(i - distance, i) for i in devices if i - distance in devices]
    return lax.ppermute(block, axis, route)


def padded_2(cells, sides, width):
    for axis, dim in sides:
        count = lax.axis_size(axis)
        ends = count - 1
        head = lax.slice_in_dim(cells, 0, width, axis=dim)
        tail = lax.slice_in_dim(cells, cells.shape[dim] - width, cells.shape[dim], axis=dim)
        cells = jnp.concatenate(
            [
                lax.ppermute(tail, axis, [(i, (i + 1) % count) for i in range(ends)]),
                cells,
                lax.ppermute(head, axis, [((i + 1) % count, i) for i in range(ends)]),
            ],
            axis=dim,
        )
    return cells


def activate(values, gain_row):
    widened = values.astype(jnp.float32)
    squares = jnp.mean(widened * widened, axis=2, keepdims=True)
    normed = widened * lax.rsqrt(squares + EPSILON) * gain_row[None, None, :, None]
    return jax.nn.silu(normed).astype(jnp.bfloat16)


def surround(values):
    trailing = passed_along(values[-2:], "tm", 1)
    joined = jnp.concatenate([trailing, values], axis=0)
    return padded_2(joined, (("rows", 1),), 1)


def convolve(padded, weight, frames, row_count):
    total = None
    for column_tap in range(3):
        partial_sum = None
        for time_tap in range(3):
            for row_tap in range(3):
                window = padded[time_tap : time_tap + frames, row_tap : row_tap + row_count]
                product = jnp.einsum(
                    "oc,fhcw->fhow",
                    weight[9 * time_tap + 3 * row_tap + column_tap],
                    window,
                    preferred_element_type=jnp.float32,
                )
                partial_sum = product if partial_sum is None else partial_sum + product
        zero_column = jnp.zeros(partial_sum.shape[:3] + (1,), jnp.float32)
        if column_tap == 0:
            partial_sum = jnp.concatenate([zero_column, partial_sum[..., :-1]], axis=3)
        elif column_tap == 2:
            partial_sum = jnp.concatenate([partial_sum[..., 1:], zero_column], axis=3)
        total = partial_sum if total is None else total + partial_sum
    return total


def on_device(latents, conv_weight, norm_gains, biases):
    values = latents
    frames = values.shape[0]
    row_count = values.shape[1]
    for layer_index in range(LAYERS):
        padded = surround(activate(values, norm_gains[layer_index]))
        total = convolve(padded, conv_weight[layer_index], frames, row_count)
        summed = values.astype(jnp.float32) + total + biases[layer_index][None, None, :, None]
        values = summed.astype(jnp.bfloat16)
    return values


def solution(mesh):
    in_specs = (P(("clips", "tm"), "rows", None, None), P(), P(), P())
    out_specs = P(("clips", "tm"), "rows", None, None)
    return jax.shard_map(
        on_device, mesh=mesh, in_specs=in_specs, out_specs=out_specs, check_vma=False
    )
```

profile of v0, /device:TPU:25, one launch (start us, length us, event | category | flops | bytes accessed | tf_op | source)
XLA Modules:
  0.0 79.3 jit_solution(3278248625686851769)
XLA Ops:
  0.0 0.9 %fusion.386 = (f32[1,192]{1,0:T(1,128)S(1)}, f32[1,192]{1,0:T(1,128)S(1)}, f32[1,192]{1,0:T(1,128)S(1)}) fusion(f32[3,192]{1,0:T(4,128)} %param.6), kind=kLoop, calls=%fused_computation.431 | loop fusion | bytes 4608 | tf_op jit(solution)/shard_map/slice | solution.py:76
  0.9 1.2 %fusion.80 = f32[4,2,128]{2,1,0:T(2,128)S(1)} fusion(bf16[4,2,192,128]{3,2,1,0:T(8,128)(2,1)} %param.4), kind=kLoop, calls=%fused_computation.115 | loop fusion | flops 588800 | bytes 397312 | tf_op jit(solution)/shard_map/reduce_sum | solution.py:37
  2.1 1.6 %fusion.87 = bf16[4,2,192,128]{3,2,1,0:T(8,128)(2,1)S(1)} fusion(bf16[4,2,192,128]{3,2,1,0:T(8,128)(2,1)} %param.4, f32[192]{0:T(256)S(1)} %bitcast.645, f32[4,2,128]{2,1,0:T(2,128)S(1)} %add_rsqrt_fusion.2), kind=kLoop, calls=%fused_computation.122 | loop fusion | flops 1572864 | bytes 791296 | tf_op jit(solution)/shard_map/convert_element_type | solution.py:39
  3.8 1.3 %collective-permute-start = (bf16[2,2,192,128]{3,2,1,0:T(8,128)(2,1)S(1)}, bf16[2,2,192,128]{3,2,1,0:T(8,128)(2,1)S(1)}, u32[]{:S(2)}, u32[]{:S(2)}) collective-permute-start(bf16[2,2,192,128]{3,2,1,0:T(8,128)(2,1)S(1)} %slice.735), channel_id=1, source_target_pairs={{0,4},{4,8},{8,12},{1,5},{5,9},{9,13},{2,6},{6,10},{10,14},{3,7},{... | collective-permute-start | bytes 589832 | tf_op jit(solution)/shard_map/ppermute | solution.py:15
  5.1 1.2 %fusion.284 = f32[4,2,128,192]{2,3,1,0:T(8,128)S(1)} fusion(bf16[4,2,192,128]{3,2,1,0:T(8,128)(2,1)S(1)} %fusion.87, bf16[3,27,192,192]{3,2,1,0:T(8,128)(2,1)} %param.5), kind=kOutput, calls=%fused_computation.335 | convolution fusion | flops 75497472 | bytes 1277952 | tf_op jit(solution)/shard_map/oc,fhcw->fhow/dot_general | solution.py:55
  6.2 1.2 %fusion.272 = f32[4,2,128,192]{2,3,1,0:T(8,128)S(1)} fusion(bf16[4,2,192,128]{3,2,1,0:T(8,128)(2,1)S(1)} %fusion.87, bf16[3,27,192,192]{3,2,1,0:T(8,128)(2,1)} %param.5), kind=kOutput, calls=%fused_computation.323 | convolution fusion | flops 75497472 | bytes 1277952 | tf_op jit(solution)/shard_map/oc,fhcw->fhow/dot_general | solution.py:55
  7.4 1.2 %fusion.260 = f32[4,2,128,192]{2,3,1,0:T(8,128)S(1)} fusion(bf16[4,2,192,128]{3,2,1,0:T(8,128)(2,1)S(1)} %fusion.87, bf16[3,27,192,192]{3,2,1,0:T(8,128)(2,1)} %param.5), kind=kOutput, calls=%fused_computation.311 | convolution fusion | flops 75497472 | bytes 1277952 | tf_op jit(solution)/shard_map/oc,fhcw->fhow/dot_general | solution.py:55
  8.5 0.8 %fusion.385 = (f32[1,192]{1,0:T(1,128)S(1)}, f32[1,192]{1,0:T(1,128)S(1)}, f32[1,192]{1,0:T(1,128)S(1)}) fusion(f32[3,192]{1,0:T(4,128)} %param.7), kind=kLoop, calls=%fused_computation.430 | loop fusion | bytes 4608 | tf_op jit(solution)/shard_map/slice | solution.py:78
  9.3 2.1 %collective-permute-done = bf16[2,2,192,128]{3,2,1,0:T(8,128)(2,1)S(1)} collective-permute-done((bf16[2,2,192,128]{3,2,1,0:T(8,128)(2,1)S(1)}, bf16[2,2,192,128]{3,2,1,0:T(8,128)(2,1)S(1)}, u32[]{:S(2)}, u32[]{:S(2)}) %collective-permute-start) | collective-permute-done | bytes 196640 | tf_op jit(solution)/shard_map/ppermute | solution.py:15
  11.5 4.6 %collective-permute-start.1 = (bf16[6,1,192,128]{3,2,1,0:T(8,128)(2,1)S(1)}, bf16[6,1,192,128]{3,2,1,0:T(8,128)(2,1)S(1)}, u32[]{:S(2)}, u32[]{:S(2)}) collective-permute-start(bf16[6,1,192,128]{3,2,1,0:T(8,128)(2,1)S(1)} %get-tuple-element.16), channel_id=1, source_target_pairs={{0,1},{1,2},{2,3},{4,5},{5,6},{6,7},{8,9},{9,10},{10,11},{12,13},{... | collective-permute-start | bytes 884744 | tf_op jit(solution)/shard_map/ppermute | solution.py:26
  16.0 1.9 %collective-permute-start.2 = (bf16[6,1,192,128]{3,2,1,0:T(8,128)(2,1)S(1)}, bf16[6,1,192,128]{3,2,1,0:T(8,128)(2,1)S(1)}, u32[]{:S(2)}, u32[]{:S(2)}) collective-permute-start(bf16[6,1,192,128]{3,2,1,0:T(8,128)(2,1)S(1)} %get-tuple-element.15), channel_id=1, source_target_pairs={{1,0},{2,1},{3,2},{5,4},{6,5},{7,6},{9,8},{10,9},{11,10},{13,12},{... | collective-permute-start | bytes 884744 | tf_op jit(solution)/shard_map/ppermute | solution.py:28
  18.0 1.2 %fusion.288 = f32[4,2,128,192]{2,3,1,0:T(8,128)S(1)} fusion(bf16[3,27,192,192]{3,2,1,0:T(8,128)(2,1)} %param.5, bf16[4,2,192,128]{3,2,1,0:T(8,128)(2,1)S(1)} %fusion.87, bf16[2,2,192,128]{3,2,1,0:T(8,128)(2,1)S(1)} %collective-permute-done), kind=kOutput, calls=%fused_computation.339 | convolution fusion | flops 76283904 | bytes 1474560 | tf_op jit(solution)/shard_map/oc,fhcw->fhow/dot_general | solution.py:55
  20.5 3.6 %collective-permute-done.2 = bf16[6,1,192,128]{3,2,1,0:T(8,128)(2,1)S(1)} collective-permute-done((bf16[6,1,192,128]{3,2,1,0:T(8,128)(2,1)S(1)}, bf16[6,1,192,128]{3,2,1,0:T(8,128)(2,1)S(1)}, u32[]{:S(2)}, u32[]{:S(2)}) %collective-permute-start.2) | collective-permute-done | bytes 294944 | tf_op jit(solution)/shard_map/ppermute | solution.py:28
  27.3 0.4 fusion.74
  28.1 0.4 fusion.56
  29.1 0.6 fusion.67
  29.6 0.5 multiply_reduce_fusion.1
  31.0 1.3 %collective-permute-start.3 = (bf16[2,2,192,128]{3,2,1,0:T(8,128)(2,1)S(1)}, bf16[2,2,192,128]{3,2,1,0:T(8,128)(2,1)S(1)}, u32[]{:S(2)}, u32[]{:S(2)}) collective-permute-start(bf16[2,2,192,128]{3,2,1,0:T(8,128)(2,1)S(1)} %slice.750), channel_id=1, source_target_pairs={{0,4},{4,8},{8,12},{1,5},{5,9},{9,13},{2,6},{6,10},{10,14},{3,7},{... | collective-permute-start | bytes 589832 | tf_op jit(solution)/shard_map/ppermute | solution.py:15
  32.5 4.9 %collective-permute-done.3 = bf16[2,2,192,128]{3,2,1,0:T(8,128)(2,1)S(1)} collective-permute-done((bf16[2,2,192,128]{3,2,1,0:T(8,128)(2,1)S(1)}, bf16[2,2,192,128]{3,2,1,0:T(8,128)(2,1)S(1)}, u32[]{:S(2)}, u32[]{:S(2)}) %collective-permute-start.3) | collective-permute-done | bytes 196640 | tf_op jit(solution)/shard_map/ppermute | solution.py:15
  37.4 2.9 %collective-permute-start.4 = (bf16[6,1,192,128]{3,2,1,0:T(8,128)(2,1)S(1)}, bf16[6,1,192,128]{3,2,1,0:T(8,128)(2,1)S(1)}, u32[]{:S(2)}, u32[]{:S(2)}) collective-permute-start(bf16[6,1,192,128]{3,2,1,0:T(8,128)(2,1)S(1)} %get-tuple-element.12), channel_id=1, source_target_pairs={{0,1},{1,2},{2,3},{4,5},{5,6},{6,7},{8,9},{9,10},{10,11},{12,13},{... | collective-permute-start | bytes 884744 | tf_op jit(solution)/shard_map/ppermute | solution.py:26
  40.3 2.1 %collective-permute-start.5 = (bf16[6,1,192,128]{3,2,1,0:T(8,128)(2,1)S(1)}, bf16[6,1,192,128]{3,2,1,0:T(8,128)(2,1)S(1)}, u32[]{:S(2)}, u32[]{:S(2)}) collective-permute-start(bf16[6,1,192,128]{3,2,1,0:T(8,128)(2,1)S(1)} %get-tuple-element.11), channel_id=1, source_target_pairs={{1,0},{2,1},{3,2},{5,4},{6,5},{7,6},{9,8},{10,9},{11,10},{13,12},{... | collective-permute-start | bytes 884744 | tf_op jit(solution)/shard_map/ppermute | solution.py:28
  44.0 4.4 %collective-permute-done.5 = bf16[6,1,192,128]{3,2,1,0:T(8,128)(2,1)S(1)} collective-permute-done((bf16[6,1,192,128]{3,2,1,0:T(8,128)(2,1)S(1)}, bf16[6,1,192,128]{3,2,1,0:T(8,128)(2,1)S(1)}, u32[]{:S(2)}, u32[]{:S(2)}) %collective-permute-start.5) | collective-permute-done | bytes 294944 | tf_op jit(solution)/shard_map/ppermute | solution.py:28
  53.3 0.6 fusion.42
  53.9 0.5 multiply_reduce_fusion
  55.2 1.3 %collective-permute-start.6 = (bf16[2,2,192,128]{3,2,1,0:T(8,128)(2,1)S(1)}, bf16[2,2,192,128]{3,2,1,0:T(8,128)(2,1)S(1)}, u32[]{:S(2)}, u32[]{:S(2)}) collective-permute-start(bf16[2,2,192,128]{3,2,1,0:T(8,128)(2,1)S(1)} %slice.765), channel_id=1, source_target_pairs={{0,4},{4,8},{8,12},{1,5},{5,9},{9,13},{2,6},{6,10},{10,14},{3,7},{... | collective-permute-start | bytes 589832 | tf_op jit(solution)/shard_map/ppermute | solution.py:15
  56.8 4.9 %collective-permute-done.6 = bf16[2,2,192,128]{3,2,1,0:T(8,128)(2,1)S(1)} collective-permute-done((bf16[2,2,192,128]{3,2,1,0:T(8,128)(2,1)S(1)}, bf16[2,2,192,128]{3,2,1,0:T(8,128)(2,1)S(1)}, u32[]{:S(2)}, u32[]{:S(2)}) %collective-permute-start.6) | collective-permute-done | bytes 196640 | tf_op jit(solution)/shard_map/ppermute | solution.py:15
  61.7 2.9 %collective-permute-start.7 = (bf16[6,1,192,128]{3,2,1,0:T(8,128)(2,1)S(1)}, bf16[6,1,192,128]{3,2,1,0:T(8,128)(2,1)S(1)}, u32[]{:S(2)}, u32[]{:S(2)}) collective-permute-start(bf16[6,1,192,128]{3,2,1,0:T(8,128)(2,1)S(1)} %get-tuple-element.8), channel_id=1, source_target_pairs={{0,1},{1,2},{2,3},{4,5},{5,6},{6,7},{8,9},{9,10},{10,11},{12,13},{... | collective-permute-start | bytes 884744 | tf_op jit(solution)/shard_map/ppermute | solution.py:26
  64.6 1.9 %collective-permute-start.8 = (bf16[6,1,192,128]{3,2,1,0:T(8,128)(2,1)S(1)}, bf16[6,1,192,128]{3,2,1,0:T(8,128)(2,1)S(1)}, u32[]{:S(2)}, u32[]{:S(2)}) collective-permute-start(bf16[6,1,192,128]{3,2,1,0:T(8,128)(2,1)S(1)} %get-tuple-element.7), channel_id=1, source_target_pairs={{1,0},{2,1},{3,2},{5,4},{6,5},{7,6},{9,8},{10,9},{11,10},{13,12},{... | collective-permute-start | bytes 884744 | tf_op jit(solution)/shard_map/ppermute | solution.py:28
  68.3 4.4 %collective-permute-done.8 = bf16[6,1,192,128]{3,2,1,0:T(8,128)(2,1)S(1)} collective-permute-done((bf16[6,1,192,128]{3,2,1,0:T(8,128)(2,1)S(1)}, bf16[6,1,192,128]{3,2,1,0:T(8,128)(2,1)S(1)}, u32[]{:S(2)}, u32[]{:S(2)}) %collective-permute-start.8) | collective-permute-done | bytes 294944 | tf_op jit(solution)/shard_map/ppermute | solution.py:28
  75.9 0.4 fusion.24
  77.6 0.6 fusion.17
  78.2 1.2 %fusion.79 = bf16[4,2,192,128]{3,2,1,0:T(8,128)(2,1)} fusion(f32[4,2,192,128]{3,2,1,0:T(8,128)S(1)} %get-tuple-element.26, f32[4,2,128,192]{2,3,1,0:T(8,128)S(1)} %fusion.17, f32[4,2,192,127]{3,2,1,0:T(8,128)S(1)} %slice.779, f32[4,2,192,127]{3,2,1,0:T(8,128)S(1)} %bitcast.641, f32[192]{0:T(256)S(1)} %bitcast.644, ...), kind=kOutput, calls=%fused_computation.97 | convolution fusion | flops 76677120 | bytes 4031488 | tf_op jit(solution)/shard_map/oc,fhcw->fhow/dot_general | solution.py:55
  (92 shorter events, 20.2 us)
Async XLA Ops:
  0.0 19.1 %copy-start = (bf16[3,27,192,192]{3,2,1,0:T(8,128)(2,1)S(1)}, bf16[3,27,192,192]{3,2,1,0:T(8,128)(2,1)}, u32[]{:S(2)}) copy-start(bf16[3,27,192,192]{3,2,1,0:T(8,128)(2,1)} %param.5) | copy-start | bytes 17915908
  3.8 7.7 %collective-permute-start = (bf16[2,2,192,128]{3,2,1,0:T(8,128)(2,1)S(1)}, bf16[2,2,192,128]{3,2,1,0:T(8,128)(2,1)S(1)}, u32[]{:S(2)}, u32[]{:S(2)}) collective-permute-start(bf16[2,2,192,128]{3,2,1,0:T(8,128)(2,1)S(1)} %slice.735), channel_id=1, source_target_pairs={{0,4},{4,8},{8,12},{1,5},{5,9},{9,13},{2,6},{6,10},{10,14},{3,7},{... | collective-permute-start | bytes 589832 | tf_op jit(solution)/shard_map/ppermute | solution.py:15
  11.5 9.0 %collective-permute-start.1 = (bf16[6,1,192,128]{3,2,1,0:T(8,128)(2,1)S(1)}, bf16[6,1,192,128]{3,2,1,0:T(8,128)(2,1)S(1)}, u32[]{:S(2)}, u32[]{:S(2)}) collective-permute-start(bf16[6,1,192,128]{3,2,1,0:T(8,128)(2,1)S(1)} %get-tuple-element.16), channel_id=1, source_target_pairs={{0,1},{1,2},{2,3},{4,5},{5,6},{6,7},{8,9},{9,10},{10,11},{12,13},{... | collective-permute-start | bytes 884744 | tf_op jit(solution)/shard_map/ppermute | solution.py:26
  16.0 8.0 %collective-permute-start.2 = (bf16[6,1,192,128]{3,2,1,0:T(8,128)(2,1)S(1)}, bf16[6,1,192,128]{3,2,1,0:T(8,128)(2,1)S(1)}, u32[]{:S(2)}, u32[]{:S(2)}) collective-permute-start(bf16[6,1,192,128]{3,2,1,0:T(8,128)(2,1)S(1)} %get-tuple-element.15), channel_id=1, source_target_pairs={{1,0},{2,1},{3,2},{5,4},{6,5},{7,6},{9,8},{10,9},{11,10},{13,12},{... | collective-permute-start | bytes 884744 | tf_op jit(solution)/shard_map/ppermute | solution.py:28
  28.1 1.6 %copy-start.1 = (bf16[4,2,192,128]{3,2,1,0:T(8,128)(2,1)S(1)}, bf16[4,2,192,128]{3,2,1,0:T(8,128)(2,1)}, u32[]{:S(2)}) copy-start(bf16[4,2,192,128]{3,2,1,0:T(8,128)(2,1)} %param.4) | copy-start | bytes 1179652
  31.0 6.4 %collective-permute-start.3 = (bf16[2,2,192,128]{3,2,1,0:T(8,128)(2,1)S(1)}, bf16[2,2,192,128]{3,2,1,0:T(8,128)(2,1)S(1)}, u32[]{:S(2)}, u32[]{:S(2)}) collective-permute-start(bf16[2,2,192,128]{3,2,1,0:T(8,128)(2,1)S(1)} %slice.750), channel_id=1, source_target_pairs={{0,4},{4,8},{8,12},{1,5},{5,9},{9,13},{2,6},{6,10},{10,14},{3,7},{... | collective-permute-start | bytes 589832 | tf_op jit(solution)/shard_map/ppermute | solution.py:15
  37.4 6.6 %collective-permute-start.4 = (bf16[6,1,192,128]{3,2,1,0:T(8,128)(2,1)S(1)}, bf16[6,1,192,128]{3,2,1,0:T(8,128)(2,1)S(1)}, u32[]{:S(2)}, u32[]{:S(2)}) collective-permute-start(bf16[6,1,192,128]{3,2,1,0:T(8,128)(2,1)S(1)} %get-tuple-element.12), channel_id=1, source_target_pairs={{0,1},{1,2},{2,3},{4,5},{5,6},{6,7},{8,9},{9,10},{10,11},{12,13},{... | collective-permute-start | bytes 884744 | tf_op jit(solution)/shard_map/ppermute | solution.py:26
  40.3 8.0 %collective-permute-start.5 = (bf16[6,1,192,128]{3,2,1,0:T(8,128)(2,1)S(1)}, bf16[6,1,192,128]{3,2,1,0:T(8,128)(2,1)S(1)}, u32[]{:S(2)}, u32[]{:S(2)}) collective-permute-start(bf16[6,1,192,128]{3,2,1,0:T(8,128)(2,1)S(1)} %get-tuple-element.11), channel_id=1, source_target_pairs={{1,0},{2,1},{3,2},{5,4},{6,5},{7,6},{9,8},{10,9},{11,10},{13,12},{... | collective-permute-start | bytes 884744 | tf_op jit(solution)/shard_map/ppermute | solution.py:28
  55.2 6.4 %collective-permute-start.6 = (bf16[2,2,192,128]{3,2,1,0:T(8,128)(2,1)S(1)}, bf16[2,2,192,128]{3,2,1,0:T(8,128)(2,1)S(1)}, u32[]{:S(2)}, u32[]{:S(2)}) collective-permute-start(bf16[2,2,192,128]{3,2,1,0:T(8,128)(2,1)S(1)} %slice.765), channel_id=1, source_target_pairs={{0,4},{4,8},{8,12},{1,5},{5,9},{9,13},{2,6},{6,10},{10,14},{3,7},{... | collective-permute-start | bytes 589832 | tf_op jit(solution)/shard_map/ppermute | solution.py:15
  61.7 6.6 %collective-permute-start.7 = (bf16[6,1,192,128]{3,2,1,0:T(8,128)(2,1)S(1)}, bf16[6,1,192,128]{3,2,1,0:T(8,128)(2,1)S(1)}, u32[]{:S(2)}, u32[]{:S(2)}) collective-permute-start(bf16[6,1,192,128]{3,2,1,0:T(8,128)(2,1)S(1)} %get-tuple-element.8), channel_id=1, source_target_pairs={{0,1},{1,2},{2,3},{4,5},{5,6},{6,7},{8,9},{9,10},{10,11},{12,13},{... | collective-permute-start | bytes 884744 | tf_op jit(solution)/shard_map/ppermute | solution.py:26
  64.6 8.0 %collective-permute-start.8 = (bf16[6,1,192,128]{3,2,1,0:T(8,128)(2,1)S(1)}, bf16[6,1,192,128]{3,2,1,0:T(8,128)(2,1)S(1)}, u32[]{:S(2)}, u32[]{:S(2)}) collective-permute-start(bf16[6,1,192,128]{3,2,1,0:T(8,128)(2,1)S(1)} %get-tuple-element.7), channel_id=1, source_target_pairs={{1,0},{2,1},{3,2},{5,4},{6,5},{7,6},{9,8},{10,9},{11,10},{13,12},{... | collective-permute-start | bytes 884744 | tf_op jit(solution)/shard_map/ppermute | solution.py:28
where the time goes:
time: 79.8 us; the launch traced here: 79.3 us
  matrix products  27.7 us (35%)
  waiting for transfers between devices  24.3 us (30%)
  starting transfers between devices  20.2 us (25%)
  other arithmetic  3.99 us (5%)
  local copies, waits for them, and re-layouts  2.54 us (3%)
    dot_general x81, matrix products, convolve(): jnp.einsum('oc,fhcw->fhow', weight[9 * time_tap + 3 * row_tap + column_ta...  27.7 us
    ppermute x3, waiting for transfers between devices, padded_2(): lax.ppermute(head, axis, [((i + 1) % count, i) for i in range(ends)])  12.4 us
    ppermute x3, waiting for transfers between devices, passed_along(): return lax.ppermute(block, axis, route)  11.8 us
    ppermute x3, starting transfers between devices, padded_2(): lax.ppermute(tail, axis, [(i, (i + 1) % count) for i in range(ends)])  10.3 us
    ppermute x3, starting transfers between devices, padded_2(): lax.ppermute(head, axis, [((i + 1) % count, i) for i in range(ends)])  5.94 us
    ppermute x3, starting transfers between devices, passed_along(): return lax.ppermute(block, axis, route)  3.88 us
    convert_element_type x3, other arithmetic, activate(): return jax.nn.silu(normed).astype(jnp.bfloat16)  2.23 us
  transfers between devices with their start and end apart: 9, of which 7 were waited for; matrix products, arithmetic and copies ran while one was open for 13% of the time, Pallas kernels for 0%

commit v1 on v0

v1 whole, which is shorter than its diff:
```python
import functools

import jax
import jax.numpy as jnp
from jax import lax
from jax.experimental import pallas as pl
from jax.experimental.pallas import tpu as pltpu
from jax.sharding import PartitionSpec as P

EPSILON = 1e-06
TIME_HALO = 2
VMEM = pl.BlockSpec(memory_space=pltpu.VMEM)
SMEM = pl.BlockSpec(memory_space=pltpu.SMEM)
LIMIT = 24 * 1024 * 1024


def column(row, width):
    return jnp.transpose(jnp.broadcast_to(row, (width, row.shape[1])))


def activated(values, gain):
    squares = jnp.mean(values * values, axis=0, keepdims=True)
    normed = values * lax.rsqrt(squares + EPSILON) * gain
    return (normed / (1.0 + jnp.exp(-normed))).astype(jnp.bfloat16)


def prepare_kernel(values_ref, gains_ref, act_ref, send_ref):
    frames, rows, _, width = values_ref.shape
    gain = column(gains_ref[0:1, :], width)
    for f in range(frames):
        for r in range(rows):
            act = activated(values_ref[f, r].astype(jnp.float32), gain)
            act_ref[f, r] = act
            if f >= frames - TIME_HALO:
                send_ref[f - (frames - TIME_HALO), r] = act


def prepare(latents, gains):
    frames, rows, channels, width = latents.shape
    return pl.pallas_call(
        prepare_kernel,
        out_shape=(
            jax.ShapeDtypeStruct(latents.shape, jnp.bfloat16),
            jax.ShapeDtypeStruct((TIME_HALO, rows, channels, width), jnp.bfloat16),
        ),
        in_specs=[VMEM] * 2,
        out_specs=(VMEM, VMEM),
        compiler_params=pltpu.CompilerParams(vmem_limit_bytes=LIMIT),
        cost_estimate=pl.CostEstimate(flops=8 * latents.size, bytes_accessed=4 * latents.size, transcendentals=latents.size),
        name="prepare",
    )(latents, gains)


def weights_kernel(w_ref, out_ref):
    _, outs, ins = w_ref.shape
    for tap in range(9):
        out_ref[:, tap * ins : (tap + 1) * ins] = w_ref[3 * tap : 3 * tap + 3].reshape(3 * outs, ins)


def weights(conv_weight):
    layers, taps, outs, ins = conv_weight.shape
    return pl.pallas_call(
        weights_kernel,
        grid=(layers,),
        out_shape=jax.ShapeDtypeStruct((layers, 3 * outs, 9 * ins), conv_weight.dtype),
        in_specs=[pl.BlockSpec((None, taps, outs, ins), lambda l: (l, 0, 0, 0))],
        out_specs=pl.BlockSpec((None, 3 * outs, 9 * ins), lambda l: (l, 0, 0)),
        compiler_params=pltpu.CompilerParams(vmem_limit_bytes=LIMIT),
        cost_estimate=pl.CostEstimate(flops=0, bytes_accessed=4 * conv_weight.size, transcendentals=0),
        name="weights",
    )(conv_weight)


def layer_kernel(
    layer, last, odd_ref, values_ref, act_ref, before_ref, pair_ref, other_ref, w_ref, biases_ref, gains_ref, *refs
):
    outs, x_ref = refs[:-1], refs[-1]
    frames, rows, channels, width = values_ref.shape
    odd = odd_ref[0] == 1
    for f in range(frames + TIME_HALO):
        pair, other = pair_ref[f], other_ref[f]
        middle = before_ref[f] if f < TIME_HALO else act_ref[f - TIME_HALO]
        lines = [jnp.where(odd, pair, other)] + [middle[r] for r in range(rows)] + [jnp.where(odd, other, pair)]
        for tap in range(3):
            for r in range(rows):
                x_ref[f, tap, :, r * width : (r + 1) * width] = lines[tap + r]
    bias = column(biases_ref[layer : layer + 1, :], width)
    lane = lax.broadcasted_iota(jnp.int32, (channels, width), 1)
    if not last:
        gain = column(gains_ref[layer + 1 : layer + 2, :], width)
    for f in range(frames):
        window = x_ref[f : f + 3].reshape(9 * channels, rows * width)
        sums = jnp.dot(w_ref[...], window, preferred_element_type=jnp.float32)
        for r in range(rows):
            part = sums[:, r * width : (r + 1) * width]
            from_left = jnp.where(lane == 0, 0.0, pltpu.roll(part[:channels], 1, 1))
            from_right = jnp.where(lane == width - 1, 0.0, pltpu.roll(part[2 * channels :], width - 1, 1))
            conv = from_left + part[channels : 2 * channels] + from_right
            total = (values_ref[f, r].astype(jnp.float32) + conv + bias).astype(jnp.bfloat16)
            outs[0][f, r] = total
            if not last:
                act = activated(total.astype(jnp.float32), gain)
                outs[1][f, r] = act
                if f >= frames - TIME_HALO:
                    outs[2][f - (frames - TIME_HALO), r] = act


def one_layer(layer, last, odd, values, act, before, pair, other, weight, biases, gains):
    frames, rows, channels, width = values.shape
    whole = jax.ShapeDtypeStruct(values.shape, jnp.bfloat16)
    send = jax.ShapeDtypeStruct((TIME_HALO, rows, channels, width), jnp.bfloat16)
    out_shape = (whole,) if last else (whole, whole, send)
    weight_spec = pl.BlockSpec((None,) + weight.shape[1:], lambda i: (layer, 0, 0))
    return pl.pallas_call(
        functools.partial(layer_kernel, layer, last),
        grid=(1,),
        out_shape=out_shape,
        in_specs=[SMEM] + [VMEM] * 5 + [weight_spec] + [VMEM] * 2,
        out_specs=(VMEM,) * len(out_shape),
        scratch_shapes=[pltpu.VMEM((frames + TIME_HALO, 3, channels, rows * width), jnp.bfloat16)],
        compiler_params=pltpu.CompilerParams(vmem_limit_bytes=LIMIT),
        cost_estimate=pl.CostEstimate(
            flops=54 * channels * values.size, bytes_accessed=2 * weight.size // 3, transcendentals=values.size
        ),
        name=f"conv_layer_{layer}",
    )(odd, values, act, before, pair, other, weight, biases, gains)


def swaps(count, first):
    pairs = [(i, i + 1) for i in range(first, count - 1, 2)]
    return pairs + [(b, a) for a, b in pairs]


def on_device(latents, conv_weight, norm_gains, biases):
    layers = conv_weight.shape[0]
    strips = lax.axis_size("rows")
    blocks = lax.axis_size("tm")
    odd = lax.rem(lax.axis_index("rows"), 2).astype(jnp.int32)
    values = latents
    act, send = prepare(latents, norm_gains)
    weight = weights(conv_weight)
    for layer in range(layers):
        before = lax.ppermute(send, "tm", [(i, i + 1) for i in range(blocks - 1)])
        top = jnp.concatenate([before[:, 0], act[:, 0]], axis=0)
        bottom = jnp.concatenate([before[:, -1], act[:, -1]], axis=0)
        pair = lax.ppermute(jnp.where(odd == 1, top, bottom), "rows", swaps(strips, 0))
        other = lax.ppermute(jnp.where(odd == 1, bottom, top), "rows", swaps(strips, 1))
        last = layer == layers - 1
        result = one_layer(layer, last, odd.reshape(1), values, act, before, pair, other, weight, biases, norm_gains)
        if not last:
            values, act, send = result
    return result[0]


def solution(mesh):
    in_specs = (P(("clips", "tm"), "rows", None, None), P(), P(), P())
    out_specs = P(("clips", "tm"), "rows", None, None)
    return jax.shard_map(on_device, mesh=mesh, in_specs=in_specs, out_specs=out_specs, check_vma=False)
```

time: 79.8 us -> 60 us (0.75)
  matrix products: 27.7 us -> 0 us
  Pallas kernels: 0 us -> 10.6 us
  other arithmetic: 3.99 us -> 0.18 us
  starting transfers between devices: 20.2 us -> 16.4 us
  local copies, waits for them, and re-layouts: 2.54 us -> 5.17 us
  waiting for transfers between devices: 24.3 us -> 26.9 us
    dot_general x81 -> x0, matrix products: 27.7 us -> none  [convolve(): jnp.einsum('oc,fhcw->fhow', weight[9 * time_tap + 3 * row_tap + column_ta...]
    pallas_call x0 -> x5, Pallas kernels: none -> 10.6 us  [the longest x3 9.19 us: one_layer(): pl.pallas_call(functools.partial(layer_kernel, layer, last), grid=(1,), o...]
    unnamed x4 -> x12, local copies, waits for them, and re-layouts: 0.01 us -> 4.96 us
    ppermute x9, starting transfers between devices: 20.2 us -> 16.4 us  [the longest x3 12.3 us: on_device(): lax.ppermute(jnp.where(odd == 1, bottom, top), 'rows', swaps(strips, 1))]
    ppermute x9, waiting for transfers between devices: 24.3 us -> 26.9 us  [the longest x3 17.9 us: on_device(): before = lax.ppermute(send, 'tm', [(i, i + 1) for i in range(blocks - 1)])]
    slice x8 -> x0, local copies, waits for them, and re-layouts: 2.53 us -> none  [the longest x1 0.87 us: on_device(): padded = surround(activate(values, norm_gains[layer_index]))]
    convert_element_type x3 -> x0, other arithmetic: 2.23 us -> none  [activate(): return jax.nn.silu(normed).astype(jnp.bfloat16)]
    reduce_sum x1 -> x0, other arithmetic: 1.21 us -> none  [activate(): squares = jnp.mean(widened * widened, axis=2, keepdims=True)]
  transfers between devices with their start and end apart: 9 -> 9, of which waited for: 7 -> 5; matrix products, arithmetic and copies ran while one was open for 13% -> 0% of each run, Pallas kernels for 0% -> 2%
where the time goes in v1:
time: 60 us; the launch traced here: 59.6 us
  waiting for transfers between devices  26.9 us (45%)
  starting transfers between devices  16.4 us (27%)
  Pallas kernels  10.6 us (18%)
  local copies, waits for them, and re-layouts  5.17 us (9%)
    ppermute x3, waiting for transfers between devices, on_device(): before = lax.ppermute(send, 'tm', [(i, i + 1) for i in range(blocks - 1)])  17.9 us
    ppermute x3, starting transfers between devices, on_device(): lax.ppermute(jnp.where(odd == 1, bottom, top), 'rows', swaps(strips, 1))  12.3 us
    pallas_call x3, Pallas kernels, one_layer(): pl.pallas_call(functools.partial(layer_kernel, layer, last), grid=(1,), o...  9.19 us
    ppermute x3, waiting for transfers between devices, on_device(): lax.ppermute(jnp.where(odd == 1, bottom, top), 'rows', swaps(strips, 1))  8.97 us
    unnamed x12, local copies, waits for them, and re-layouts  4.96 us
    ppermute x3, starting transfers between devices, on_device(): before = lax.ppermute(send, 'tm', [(i, i + 1) for i in range(blocks - 1)])  3.88 us
  transfers between devices with their start and end apart: 9, of which 5 were waited for; matrix products, arithmetic and copies ran while one was open for 0% of the time, Pallas kernels for 2%

profile of v1, /device:TPU:25, one launch (start us, length us, event | category | flops | bytes accessed | tf_op | source)
XLA Modules:
  0.0 59.6 jit_solution(12928017146839801319)
XLA Ops:
  0.0 1.0 %copy-done.1 = bf16[4,2,192,128]{3,2,1,0:T(8,128)(2,1)S(1)} copy-done((bf16[4,2,192,128]{3,2,1,0:T(8,128)(2,1)S(1)}, bf16[4,2,192,128]{3,2,1,0:T(8,128)(2,1)}, u32[]{:S(2)}) %copy-start.1) | copy-done | bytes 393240
  1.0 0.7 %copy-done.3 = f32[3,192]{1,0:T(4,128)S(1)} copy-done((f32[3,192]{1,0:T(4,128)S(1)}, f32[3,192]{1,0:T(4,128)}, u32[]{:S(2)}) %copy-start.3) | copy-done | bytes 2328
  1.7 0.3 prepare.1
  2.0 1.3 %collective-permute-start = (bf16[2,2,192,128]{3,2,0,1:T(8,128)(2,1)S(1)}, bf16[2,2,192,128]{3,2,0,1:T(8,128)(2,1)S(1)}, u32[]{:S(2)}, u32[]{:S(2)}) collective-permute-start(bf16[2,2,192,128]{3,2,0,1:T(8,128)(2,1)S(1)} %copy.5), channel_id=1, source_target_pairs={{0,4},{4,8},{8,12},{1,5},{5,9},{9,13},{2,6},{6,10},{10,14},{3,7},{... | collective-permute-start | bytes 589832 | tf_op jit(solution)/shard_map/ppermute | solution.py:143
  3.4 6.3 %collective-permute-done = bf16[2,2,192,128]{3,2,0,1:T(8,128)(2,1)S(1)} collective-permute-done((bf16[2,2,192,128]{3,2,0,1:T(8,128)(2,1)S(1)}, bf16[2,2,192,128]{3,2,0,1:T(8,128)(2,1)S(1)}, u32[]{:S(2)}, u32[]{:S(2)}) %collective-permute-start) | collective-permute-done | bytes 196640 | tf_op jit(solution)/shard_map/ppermute | solution.py:143
  9.7 0.0 copy-start.2
  9.7 0.0 copy-start.4
  9.7 0.0 copy-start.5
  9.7 0.1 broadcast_select_fusion.4
  9.8 4.7 %collective-permute-start.2 = (bf16[6,192,128]{2,1,0:T(8,128)(2,1)S(1)}, bf16[6,192,128]{2,1,0:T(8,128)(2,1)S(1)}, u32[]{:S(2)}, u32[]{:S(2)}) collective-permute-start(bf16[6,192,128]{2,1,0:T(8,128)(2,1)S(1)} %get-tuple-element.25), channel_id=1, source_target_pairs={{1,2},{2,1},{5,6},{6,5},{9,10},{10,9},{13,14},{14,13},{17,18},{18,... | collective-permute-start | bytes 884744 | tf_op jit(solution)/shard_map/ppermute | solution.py:147
  14.5 0.1 collective-permute-start.1
  14.6 0.0 copy-start
  14.6 3.3 %copy-done = bf16[3,27,192,192]{3,2,1,0:T(8,128)(2,1)S(1)} copy-done((bf16[3,27,192,192]{3,2,1,0:T(8,128)(2,1)S(1)}, bf16[3,27,192,192]{3,2,1,0:T(8,128)(2,1)}, u32[]{:S(2)}) %copy-start) | copy-done | bytes 5971992
  17.8 1.1 %weights.1.w_ref = bf16[3,576,1728]{2,1,0:T(8,128)(2,1)S(1)} custom-call(bf16[3,27,192,192]{3,2,1,0:T(8,128)(2,1)S(1)} %copy-done), custom_call_target="tpu_custom_call" | custom-call | bytes 11943936 | tf_op jit(solution)/shard_map/weights/pallas_call | solution.py:62
  19.0 0.0 collective-permute-done.1.pair_ref
  19.1 2.9 %conv_layer_0.1 = (bf16[4,2,192,128]{3,2,1,0:T(8,128)(2,1)S(1)}, bf16[4,2,192,128]{3,2,1,0:T(8,128)(2,1)S(1)}, bf16[2,2,192,128]{3,2,1,0:T(8,128)(2,1)S(1)}) custom-call(s32[1]{0:T(128)} %bitcast.odd_ref, bf16[4,2,192,128]{3,2,1,0:T(8,128)(2,1)S(1)} %copy-done.2, bf16[4,2,192,128]{3,2,1,0:T(8,128)(2,1)S(1)} %get-tuple-element.13.act_ref, ...), custom_call_target="tpu_custom_call" | custom-call | flops 2038431744 | bytes 1990656 | tf_op jit(solution)/shard_map/conv_layer_0/pallas_call | solution.py:114
  22.0 1.3 %collective-permute-start.3 = (bf16[2,2,192,128]{3,2,0,1:T(8,128)(2,1)S(1)}, bf16[2,2,192,128]{3,2,0,1:T(8,128)(2,1)S(1)}, u32[]{:S(2)}, u32[]{:S(2)}) collective-permute-start(bf16[2,2,192,128]{3,2,0,1:T(8,128)(2,1)S(1)} %copy.9), channel_id=1, source_target_pairs={{0,4},{4,8},{8,12},{1,5},{5,9},{9,13},{2,6},{6,10},{10,14},{3,7},{... | collective-permute-start | bytes 589832 | tf_op jit(solution)/shard_map/ppermute | solution.py:143
  23.3 6.5 %collective-permute-done.3 = bf16[2,2,192,128]{3,2,0,1:T(8,128)(2,1)S(1)} collective-permute-done((bf16[2,2,192,128]{3,2,0,1:T(8,128)(2,1)S(1)}, bf16[2,2,192,128]{3,2,0,1:T(8,128)(2,1)S(1)}, u32[]{:S(2)}, u32[]{:S(2)}) %collective-permute-start.3) | collective-permute-done | bytes 196640 | tf_op jit(solution)/shard_map/ppermute | solution.py:143
  29.9 0.1 broadcast_select_fusion.2
  30.0 3.3 %collective-permute-start.5 = (bf16[6,192,128]{2,1,0:T(8,128)(2,1)S(1)}, bf16[6,192,128]{2,1,0:T(8,128)(2,1)S(1)}, u32[]{:S(2)}, u32[]{:S(2)}) collective-permute-start(bf16[6,192,128]{2,1,0:T(8,128)(2,1)S(1)} %get-tuple-element.23), channel_id=1, source_target_pairs={{1,2},{2,1},{5,6},{6,5},{9,10},{10,9},{13,14},{14,13},{17,18},{18,... | collective-permute-start | bytes 884744 | tf_op jit(solution)/shard_map/ppermute | solution.py:147
  33.2 0.1 collective-permute-start.4
  33.3 4.7 %collective-permute-done.5.other_ref = bf16[6,192,128]{2,1,0:T(8,128)(2,1)S(1)} collective-permute-done((bf16[6,192,128]{2,1,0:T(8,128)(2,1)S(1)}, bf16[6,192,128]{2,1,0:T(8,128)(2,1)S(1)}, u32[]{:S(2)}, u32[]{:S(2)}) %collective-permute-start.5) | collective-permute-done | bytes 294944 | tf_op jit(solution)/shard_map/ppermute | solution.py:147
  38.0 0.0 collective-permute-done.4.pair_ref
  38.0 2.9 %conv_layer_1.1 = (bf16[4,2,192,128]{3,2,1,0:T(8,128)(2,1)S(1)}, bf16[4,2,192,128]{3,2,1,0:T(8,128)(2,1)S(1)}, bf16[2,2,192,128]{3,2,1,0:T(8,128)(2,1)S(1)}) custom-call(s32[1]{0:T(128)} %bitcast.odd_ref, bf16[4,2,192,128]{3,2,1,0:T(8,128)(2,1)S(1)} %get-tuple-element.15.values_ref, bf16[4,2,192,128]{3,2,1,0:T(8,128)(2,1)S(1)} %get-tuple-element.16.act_ref, ...), custom_call_target="tpu_custom_call" | custom-call | flops 2038431744 | bytes 1990656 | tf_op jit(solution)/shard_map/conv_layer_1/pallas_call | solution.py:114
  40.9 1.3 %collective-permute-start.6 = (bf16[2,2,192,128]{3,2,0,1:T(8,128)(2,1)S(1)}, bf16[2,2,192,128]{3,2,0,1:T(8,128)(2,1)S(1)}, u32[]{:S(2)}, u32[]{:S(2)}) collective-permute-start(bf16[2,2,192,128]{3,2,0,1:T(8,128)(2,1)S(1)} %copy.13), channel_id=1, source_target_pairs={{0,4},{4,8},{8,12},{1,5},{5,9},{9,13},{2,6},{6,10},{10,14},{3,7},{... | collective-permute-start | bytes 589832 | tf_op jit(solution)/shard_map/ppermute | solution.py:143
  42.3 5.1 %collective-permute-done.6 = bf16[2,2,192,128]{3,2,0,1:T(8,128)(2,1)S(1)} collective-permute-done((bf16[2,2,192,128]{3,2,0,1:T(8,128)(2,1)S(1)}, bf16[2,2,192,128]{3,2,0,1:T(8,128)(2,1)S(1)}, u32[]{:S(2)}, u32[]{:S(2)}) %collective-permute-start.6) | collective-permute-done | bytes 196640 | tf_op jit(solution)/shard_map/ppermute | solution.py:143
  47.4 0.1 broadcast_select_fusion
  47.4 4.4 %collective-permute-start.8 = (bf16[6,192,128]{2,1,0:T(8,128)(2,1)S(1)}, bf16[6,192,128]{2,1,0:T(8,128)(2,1)S(1)}, u32[]{:S(2)}, u32[]{:S(2)}) collective-permute-start(bf16[6,192,128]{2,1,0:T(8,128)(2,1)S(1)} %get-tuple-element.21), channel_id=1, source_target_pairs={{1,2},{2,1},{5,6},{6,5},{9,10},{10,9},{13,14},{14,13},{17,18},{18,... | collective-permute-start | bytes 884744 | tf_op jit(solution)/shard_map/ppermute | solution.py:147
  51.8 0.1 collective-permute-start.7
  51.9 4.3 %collective-permute-done.8.other_ref = bf16[6,192,128]{2,1,0:T(8,128)(2,1)S(1)} collective-permute-done((bf16[6,192,128]{2,1,0:T(8,128)(2,1)S(1)}, bf16[6,192,128]{2,1,0:T(8,128)(2,1)S(1)}, u32[]{:S(2)}, u32[]{:S(2)}) %collective-permute-start.8) | collective-permute-done | bytes 294944 | tf_op jit(solution)/shard_map/ppermute | solution.py:147
  56.2 0.0 collective-permute-done.7.pair_ref
  56.2 3.4 %conv_layer_2.1 = bf16[4,2,192,128]{3,2,1,0:T(8,128)(2,1)} custom-call(s32[1]{0:T(128)} %bitcast.odd_ref, bf16[4,2,192,128]{3,2,1,0:T(8,128)(2,1)S(1)} %get-tuple-element.18.values_ref, bf16[4,2,192,128]{3,2,1,0:T(8,128)(2,1)S(1)} %get-tuple-element.19.act_ref, bf16[2,2,192,128]{3,2,1,0:T(8,128)(2,1)S(1)} %copy.16.before_ref, ...), custom_call_target="tpu_custom_call" | custom-call | flops 2038431744 | bytes 1990656 | tf_op jit(solution)/shard_map/conv_layer_2/pallas_call | solution.py:114
  (18 shorter events, 0.2 us)
Async XLA Ops:
  0.0 1.0 %copy-start.1 = (bf16[4,2,192,128]{3,2,1,0:T(8,128)(2,1)S(1)}, bf16[4,2,192,128]{3,2,1,0:T(8,128)(2,1)}, u32[]{:S(2)}) copy-start(bf16[4,2,192,128]{3,2,1,0:T(8,128)(2,1)} %values_ref.3) | copy-start | bytes 1179652
  1.0 0.7 %copy-start.3 = (f32[3,192]{1,0:T(4,128)S(1)}, f32[3,192]{1,0:T(4,128)}, u32[]{:S(2)}) copy-start(f32[3,192]{1,0:T(4,128)} %gains_ref.7) | copy-start | bytes 6916
  2.0 7.7 %collective-permute-start = (bf16[2,2,192,128]{3,2,0,1:T(8,128)(2,1)S(1)}, bf16[2,2,192,128]{3,2,0,1:T(8,128)(2,1)S(1)}, u32[]{:S(2)}, u32[]{:S(2)}) collective-permute-start(bf16[2,2,192,128]{3,2,0,1:T(8,128)(2,1)S(1)} %copy.5), channel_id=1, source_target_pairs={{0,4},{4,8},{8,12},{1,5},{5,9},{9,13},{2,6},{6,10},{10,14},{3,7},{... | collective-permute-start | bytes 589832 | tf_op jit(solution)/shard_map/ppermute | solution.py:143
  9.7 9.3 %copy-start.2 = (bf16[4,2,192,128]{3,2,1,0:T(8,128)(2,1)S(1)}, bf16[4,2,192,128]{3,2,1,0:T(8,128)(2,1)}, u32[]{:S(2)}) copy-start(bf16[4,2,192,128]{3,2,1,0:T(8,128)(2,1)} %values_ref.3) | copy-start | bytes 1179652
  9.7 9.3 %copy-start.4 = (f32[3,192]{1,0:T(4,128)S(1)}, f32[3,192]{1,0:T(4,128)}, u32[]{:S(2)}) copy-start(f32[3,192]{1,0:T(4,128)} %gains_ref.7) | copy-start | bytes 6916
  9.7 9.3 %copy-start.5 = (f32[3,192]{1,0:T(4,128)S(1)}, f32[3,192]{1,0:T(4,128)}, u32[]{:S(2)}) copy-start(f32[3,192]{1,0:T(4,128)} %biases_ref.5) | copy-start | bytes 6916
  9.8 9.2 %collective-permute-start.2 = (bf16[6,192,128]{2,1,0:T(8,128)(2,1)S(1)}, bf16[6,192,128]{2,1,0:T(8,128)(2,1)S(1)}, u32[]{:S(2)}, u32[]{:S(2)}) collective-permute-start(bf16[6,192,128]{2,1,0:T(8,128)(2,1)S(1)} %get-tuple-element.25), channel_id=1, source_target_pairs={{1,2},{2,1},{5,6},{6,5},{9,10},{10,9},{13,14},{14,13},{17,18},{18,... | collective-permute-start | bytes 884744 | tf_op jit(solution)/shard_map/ppermute | solution.py:147
  14.5 4.5 %collective-permute-start.1 = (bf16[6,192,128]{2,1,0:T(8,128)(2,1)S(1)}, bf16[6,192,128]{2,1,0:T(8,128)(2,1)S(1)}, u32[]{:S(2)}, u32[]{:S(2)}) collective-permute-start(bf16[6,192,128]{2,1,0:T(8,128)(2,1)S(1)} %get-tuple-element.26), channel_id=1, source_target_pairs={{0,1},{2,3},{1,0},{3,2},{4,5},{6,7},{5,4},{7,6},{8,9},{10,11},{9,8... | collective-permute-start | bytes 884744 | tf_op jit(solution)/shard_map/ppermute | solution.py:146
  14.6 3.3 %copy-start = (bf16[3,27,192,192]{3,2,1,0:T(8,128)(2,1)S(1)}, bf16[3,27,192,192]{3,2,1,0:T(8,128)(2,1)}, u32[]{:S(2)}) copy-start(bf16[3,27,192,192]{3,2,1,0:T(8,128)(2,1)} %w_ref.1) | copy-start | bytes 17915908
  22.0 7.9 %collective-permute-start.3 = (bf16[2,2,192,128]{3,2,0,1:T(8,128)(2,1)S(1)}, bf16[2,2,192,128]{3,2,0,1:T(8,128)(2,1)S(1)}, u32[]{:S(2)}, u32[]{:S(2)}) collective-permute-start(bf16[2,2,192,128]{3,2,0,1:T(8,128)(2,1)S(1)} %copy.9), channel_id=1, source_target_pairs={{0,4},{4,8},{8,12},{1,5},{5,9},{9,13},{2,6},{6,10},{10,14},{3,7},{... | collective-permute-start | bytes 589832 | tf_op jit(solution)/shard_map/ppermute | solution.py:143
  30.0 8.0 %collective-permute-start.5 = (bf16[6,192,128]{2,1,0:T(8,128)(2,1)S(1)}, bf16[6,192,128]{2,1,0:T(8,128)(2,1)S(1)}, u32[]{:S(2)}, u32[]{:S(2)}) collective-permute-start(bf16[6,192,128]{2,1,0:T(8,128)(2,1)S(1)} %get-tuple-element.23), channel_id=1, source_target_pairs={{1,2},{2,1},{5,6},{6,5},{9,10},{10,9},{13,14},{14,13},{17,18},{18,... | collective-permute-start | bytes 884744 | tf_op jit(solution)/shard_map/ppermute | solution.py:147
  33.2 4.8 %collective-permute-start.4 = (bf16[6,192,128]{2,1,0:T(8,128)(2,1)S(1)}, bf16[6,192,128]{2,1,0:T(8,128)(2,1)S(1)}, u32[]{:S(2)}, u32[]{:S(2)}) collective-permute-start(bf16[6,192,128]{2,1,0:T(8,128)(2,1)S(1)} %get-tuple-element.24), channel_id=1, source_target_pairs={{0,1},{2,3},{1,0},{3,2},{4,5},{6,7},{5,4},{7,6},{8,9},{10,11},{9,8... | collective-permute-start | bytes 884744 | tf_op jit(solution)/shard_map/ppermute | solution.py:146
  40.9 6.4 %collective-permute-start.6 = (bf16[2,2,192,128]{3,2,0,1:T(8,128)(2,1)S(1)}, bf16[2,2,192,128]{3,2,0,1:T(8,128)(2,1)S(1)}, u32[]{:S(2)}, u32[]{:S(2)}) collective-permute-start(bf16[2,2,192,128]{3,2,0,1:T(8,128)(2,1)S(1)} %copy.13), channel_id=1, source_target_pairs={{0,4},{4,8},{8,12},{1,5},{5,9},{9,13},{2,6},{6,10},{10,14},{3,7},{... | collective-permute-start | bytes 589832 | tf_op jit(solution)/shard_map/ppermute | solution.py:143
  47.4 8.8 %collective-permute-start.8 = (bf16[6,192,128]{2,1,0:T(8,128)(2,1)S(1)}, bf16[6,192,128]{2,1,0:T(8,128)(2,1)S(1)}, u32[]{:S(2)}, u32[]{:S(2)}) collective-permute-start(bf16[6,192,128]{2,1,0:T(8,128)(2,1)S(1)} %get-tuple-element.21), channel_id=1, source_target_pairs={{1,2},{2,1},{5,6},{6,5},{9,10},{10,9},{13,14},{14,13},{17,18},{18,... | collective-permute-start | bytes 884744 | tf_op jit(solution)/shard_map/ppermute | solution.py:147
  51.8 4.4 %collective-permute-start.7 = (bf16[6,192,128]{2,1,0:T(8,128)(2,1)S(1)}, bf16[6,192,128]{2,1,0:T(8,128)(2,1)S(1)}, u32[]{:S(2)}, u32[]{:S(2)}) collective-permute-start(bf16[6,192,128]{2,1,0:T(8,128)(2,1)S(1)} %get-tuple-element.22), channel_id=1, source_target_pairs={{0,1},{2,3},{1,0},{3,2},{4,5},{6,7},{5,4},{7,6},{8,9},{10,11},{9,8... | collective-permute-start | bytes 884744 | tf_op jit(solution)/shard_map/ppermute | solution.py:146

commit v2 on v1

--- a/solution.py
+++ b/solution.py
@@ -77,8 +77,10 @@
     outs, x_ref = refs[:-1], refs[-1]
     frames, rows, channels, width = values_ref.shape
     odd = odd_ref[0] == 1
+    pair_zero = jnp.zeros((channels, width), jnp.bfloat16)
     for f in range(frames + TIME_HALO):
-        pair, other = pair_ref[f], other_ref[f]
+        pair = pair_ref[1 - odd_ref[0], f]
+        other = jnp.where(odd_ref[1] == 1, pair_zero, other_ref[odd_ref[0], f])
         middle = before_ref[f] if f < TIME_HALO else act_ref[f - TIME_HALO]
         lines = [jnp.where(odd, pair, other)] + [middle[r] for r in range(rows)] + [jnp.where(odd, other, pair)]
         for tap in range(3):
@@ -126,27 +128,29 @@
     )(odd, values, act, before, pair, other, weight, biases, gains)
 
 
-def swaps(count, first):
-    pairs = [(i, i + 1) for i in range(first, count - 1, 2)]
-    return pairs + [(b, a) for a, b in pairs]
-
-
 def on_device(latents, conv_weight, norm_gains, biases):
     layers = conv_weight.shape[0]
     strips = lax.axis_size("rows")
     blocks = lax.axis_size("tm")
-    odd = lax.rem(lax.axis_index("rows"), 2).astype(jnp.int32)
+    strip = lax.axis_index("rows")
+    odd = lax.rem(strip, 2).astype(jnp.int32)
+    edge = ((strip == 0) | (strip == strips - 1)).astype(jnp.int32)
+    place = jnp.stack([odd, edge])
+    pairs = [[i, i + 1] for i in range(0, strips, 2)]
+    others = [[i, (i + 1) % strips] for i in range(1, strips, 2)]
     values = latents
     act, send = prepare(latents, norm_gains)
     weight = weights(conv_weight)
     for layer in range(layers):
         before = lax.ppermute(send, "tm", [(i, i + 1) for i in range(blocks - 1)])
+        if layer == 0:
+            before, weight = lax.optimization_barrier((before, weight))
         top = jnp.concatenate([before[:, 0], act[:, 0]], axis=0)
         bottom = jnp.concatenate([before[:, -1], act[:, -1]], axis=0)
-        pair = lax.ppermute(jnp.where(odd == 1, top, bottom), "rows", swaps(strips, 0))
-        other = lax.ppermute(jnp.where(odd == 1, bottom, top), "rows", swaps(strips, 1))
+        pair = lax.all_gather(jnp.where(odd == 1, top, bottom), "rows", axis_index_groups=pairs)
+        other = lax.all_gather(jnp.where(odd == 1, bottom, top), "rows", axis_index_groups=others)
         last = layer == layers - 1
-        result = one_layer(layer, last, odd.reshape(1), values, act, before, pair, other, weight, biases, norm_gains)
+        result = one_layer(layer, last, place, values, act, before, pair, other, weight, biases, norm_gains)
         if not last:
             values, act, send = result
     return result[0]

time: 60 us -> 76 us (1.27)
  the two profiles are of different devices: /device:TPU:25 before, /device:TPU:0 now
where the time goes in v2:
time: 76 us; the launch traced here: 75.7 us
  blocking collectives  35.7 us (47%)
  starting transfers between devices  13.3 us (18%)
  Pallas kernels  12.4 us (16%)
  waiting for transfers between devices  8.81 us (12%)
  local copies, waits for them, and re-layouts  5.1 us (7%)
    all_gather x3, blocking collectives, on_device(): lax.all_gather(jnp.where(odd == 1, bottom, top), 'rows', axis_index_group...  29 us
    ppermute x3, starting transfers between devices, on_device(): before = lax.ppermute(send, 'tm', [(i, i + 1) for i in range(blocks - 1)])  13.3 us
    pallas_call x3, Pallas kernels, one_layer(): pl.pallas_call(functools.partial(layer_kernel, layer, last), grid=(1,), o...  10.9 us
    ppermute x3, waiting for transfers between devices, on_device(): before = lax.ppermute(send, 'tm', [(i, i + 1) for i in range(blocks - 1)])  8.81 us
    all_gather x3, blocking collectives, on_device(): lax.all_gather(jnp.where(odd == 1, top, bottom), 'rows', axis_index_group...  6.65 us
    unnamed x12, local copies, waits for them, and re-layouts  4.95 us
  transfers between devices with their start and end apart: 3, of which 2 were waited for; matrix products, arithmetic and copies ran while one was open for 0% of the time, Pallas kernels for 1%

profile of v2, /device:TPU:0, one launch (start us, length us, event | category | flops | bytes accessed | tf_op | source)
XLA Modules:
  0.0 75.7 jit_solution(11592094249298782535)
XLA Ops:
  0.0 0.0 copy-start.1
  0.0 1.0 %copy-done.1 = bf16[4,2,192,128]{3,2,1,0:T(8,128)(2,1)S(1)} copy-done((bf16[4,2,192,128]{3,2,1,0:T(8,128)(2,1)S(1)}, bf16[4,2,192,128]{3,2,1,0:T(8,128)(2,1)}, u32[]{:S(2)}) %copy-start.1) | copy-done | bytes 393240
  1.0 0.0 copy-start.3
  1.0 0.7 copy-done.3
  1.7 0.3 prepare.1
  2.0 4.9 %collective-permute-start = (bf16[2,2,192,128]{3,2,0,1:T(8,128)(2,1)S(1)}, bf16[2,2,192,128]{3,2,0,1:T(8,128)(2,1)S(1)}, u32[]{:S(2)}, u32[]{:S(2)}) collective-permute-start(bf16[2,2,192,128]{3,2,0,1:T(8,128)(2,1)S(1)} %copy.17), channel_id=1, source_target_pairs={{0,4},{4,8},{8,12},{1,5},{5,9},{9,13},{2,6},{6,10},{10,14},{3,7},{... | collective-permute-start | bytes 589832 | tf_op jit(solution)/shard_map/ppermute | solution.py:145
  7.0 0.0 copy-start
  7.0 3.3 %copy-done = bf16[3,27,192,192]{3,2,1,0:T(8,128)(2,1)S(1)} copy-done((bf16[3,27,192,192]{3,2,1,0:T(8,128)(2,1)S(1)}, bf16[3,27,192,192]{3,2,1,0:T(8,128)(2,1)}, u32[]{:S(2)}) %copy-start) | copy-done | bytes 5971992
  10.3 0.0 copy-start.2
  10.3 0.0 copy-start.4
  10.3 1.1 %weights.1.w_ref = bf16[3,576,1728]{2,1,0:T(8,128)(2,1)S(1)} custom-call(bf16[3,27,192,192]{3,2,1,0:T(8,128)(2,1)S(1)} %copy-done), custom_call_target="tpu_custom_call" | custom-call | bytes 11943936 | tf_op jit(solution)/shard_map/weights/pallas_call | solution.py:62
  11.4 0.1 pad_add_fusion.odd_ref
  11.5 0.0 collective-permute-done
  11.6 0.1 broadcast_select_fusion.4
  11.6 9.9 %all_gather.25.other_ref = bf16[2,6,192,128]{3,2,1,0:T(8,128)(2,1)S(1)} all-gather(bf16[1,6,192,128]{3,2,1,0:T(8,128)(2,1)S(1)} %get-tuple-element.29), channel_id=1, replica_groups={{1,2},{3,0},{5,6},{7,4},{9,10},{11,8},{13,14},{15,12},{17,18},{19,16},{..., dimensions={0}, use_global_device_ids=true | all-gather | bytes 884736 | tf_op jit(solution)/shard_map/all_gather | solution.py:151
  21.6 2.2 %all_gather.24.pair_ref = bf16[2,6,192,128]{3,2,1,0:T(8,128)(2,1)S(1)} all-gather(bf16[1,6,192,128]{3,2,1,0:T(8,128)(2,1)S(1)} %get-tuple-element.30), channel_id=1, replica_groups={{0,1},{2,3},{4,5},{6,7},{8,9},{10,11},{12,13},{14,15},{16,17},{18,19},{..., dimensions={0}, use_global_device_ids=true | all-gather | bytes 884736 | tf_op jit(solution)/shard_map/all_gather | solution.py:150
  23.8 0.0 copy-done.2
  23.8 0.0 copy-done.4
  23.8 0.0 copy-done.5
  23.8 3.5 %conv_layer_0.1 = (bf16[4,2,192,128]{3,2,1,0:T(8,128)(2,1)S(1)}, bf16[4,2,192,128]{3,2,1,0:T(8,128)(2,1)S(1)}, bf16[2,2,192,128]{3,2,1,0:T(8,128)(2,1)S(1)}) custom-call(s32[2]{0:T(128)S(1)} %pad_add_fusion.odd_ref, bf16[4,2,192,128]{3,2,1,0:T(8,128)(2,1)S(1)} %copy-done.2, bf16[4,2,192,128]{3,2,1,0:T(8,128)(2,1)S(1)} %get-tuple-element.15.act_ref, ...), custom_call_target="tpu_custom_call" | custom-call | flops 2038431744 | bytes 1990656 | tf_op jit(solution)/shard_map/conv_layer_0/pallas_call | solution.py:116
  27.3 4.0 %collective-permute-start.1 = (bf16[2,2,192,128]{3,2,1,0:T(8,128)(2,1)S(1)}, bf16[2,2,192,128]{3,2,1,0:T(8,128)(2,1)S(1)}, u32[]{:S(2)}, u32[]{:S(2)}) collective-permute-start(bf16[2,2,192,128]{3,2,1,0:T(8,128)(2,1)S(1)} %get-tuple-element.21), channel_id=1, source_target_pairs={{0,4},{4,8},{8,12},{1,5},{5,9},{9,13},{2,6},{6,10},{10,14},{3,7},{... | collective-permute-start | bytes 589832 | tf_op jit(solution)/shard_map/ppermute | solution.py:145
  31.3 4.4 %collective-permute-done.1.before_ref = bf16[2,2,192,128]{3,2,1,0:T(8,128)(2,1)S(1)} collective-permute-done((bf16[2,2,192,128]{3,2,1,0:T(8,128)(2,1)S(1)}, bf16[2,2,192,128]{3,2,1,0:T(8,128)(2,1)S(1)}, u32[]{:S(2)}, u32[]{:S(2)}) %collective-permute-start.1) | collective-permute-done | bytes 196640 | tf_op jit(solution)/shard_map/ppermute | solution.py:145
  35.7 0.1 broadcast_select_fusion.2
  35.8 9.5 %all_gather.27.other_ref = bf16[2,6,192,128]{3,2,1,0:T(8,128)(2,1)S(1)} all-gather(bf16[1,6,192,128]{3,2,1,0:T(8,128)(2,1)S(1)} %get-tuple-element.27), channel_id=1, replica_groups={{1,2},{3,0},{5,6},{7,4},{9,10},{11,8},{13,14},{15,12},{17,18},{19,16},{..., dimensions={0}, use_global_device_ids=true | all-gather | bytes 884736 | tf_op jit(solution)/shard_map/all_gather | solution.py:151
  45.3 2.2 %all_gather.26.pair_ref = bf16[2,6,192,128]{3,2,1,0:T(8,128)(2,1)S(1)} all-gather(bf16[1,6,192,128]{3,2,1,0:T(8,128)(2,1)S(1)} %get-tuple-element.28), channel_id=1, replica_groups={{0,1},{2,3},{4,5},{6,7},{8,9},{10,11},{12,13},{14,15},{16,17},{18,19},{..., dimensions={0}, use_global_device_ids=true | all-gather | bytes 884736 | tf_op jit(solution)/shard_map/all_gather | solution.py:150
  47.5 3.5 %conv_layer_1.1 = (bf16[4,2,192,128]{3,2,1,0:T(8,128)(2,1)S(1)}, bf16[4,2,192,128]{3,2,1,0:T(8,128)(2,1)S(1)}, bf16[2,2,192,128]{3,2,1,0:T(8,128)(2,1)S(1)}) custom-call(s32[2]{0:T(128)S(1)} %pad_add_fusion.odd_ref, bf16[4,2,192,128]{3,2,1,0:T(8,128)(2,1)S(1)} %get-tuple-element.19.values_ref, bf16[4,2,192,128]{3,2,1,0:T(8,128)(2,1)S(1)} %get-tuple-element.20.act_ref, ...), custom_call_target="tpu_custom_call" | custom-call | flops 2038431744 | bytes 1990656 | tf_op jit(solution)/shard_map/conv_layer_1/pallas_call | solution.py:116
  51.0 4.4 %collective-permute-start.2 = (bf16[2,2,192,128]{3,2,1,0:T(8,128)(2,1)S(1)}, bf16[2,2,192,128]{3,2,1,0:T(8,128)(2,1)S(1)}, u32[]{:S(2)}, u32[]{:S(2)}) collective-permute-start(bf16[2,2,192,128]{3,2,1,0:T(8,128)(2,1)S(1)} %get-tuple-element.24), channel_id=1, source_target_pairs={{0,4},{4,8},{8,12},{1,5},{5,9},{9,13},{2,6},{6,10},{10,14},{3,7},{... | collective-permute-start | bytes 589832 | tf_op jit(solution)/shard_map/ppermute | solution.py:145
  55.4 4.4 %collective-permute-done.2.before_ref = bf16[2,2,192,128]{3,2,1,0:T(8,128)(2,1)S(1)} collective-permute-done((bf16[2,2,192,128]{3,2,1,0:T(8,128)(2,1)S(1)}, bf16[2,2,192,128]{3,2,1,0:T(8,128)(2,1)S(1)}, u32[]{:S(2)}, u32[]{:S(2)}) %collective-permute-start.2) | collective-permute-done | bytes 196640 | tf_op jit(solution)/shard_map/ppermute | solution.py:145
  59.8 0.1 broadcast_select_fusion
  59.9 9.6 %all_gather.29.other_ref = bf16[2,6,192,128]{3,2,1,0:T(8,128)(2,1)S(1)} all-gather(bf16[1,6,192,128]{3,2,1,0:T(8,128)(2,1)S(1)} %get-tuple-element.25), channel_id=1, replica_groups={{1,2},{3,0},{5,6},{7,4},{9,10},{11,8},{13,14},{15,12},{17,18},{19,16},{..., dimensions={0}, use_global_device_ids=true | all-gather | bytes 884736 | tf_op jit(solution)/shard_map/all_gather | solution.py:151
  69.5 2.2 %all_gather.28.pair_ref = bf16[2,6,192,128]{3,2,1,0:T(8,128)(2,1)S(1)} all-gather(bf16[1,6,192,128]{3,2,1,0:T(8,128)(2,1)S(1)} %get-tuple-element.26), channel_id=1, replica_groups={{0,1},{2,3},{4,5},{6,7},{8,9},{10,11},{12,13},{14,15},{16,17},{18,19},{..., dimensions={0}, use_global_device_ids=true | all-gather | bytes 884736 | tf_op jit(solution)/shard_map/all_gather | solution.py:150
  71.7 3.9 %conv_layer_2.1 = bf16[4,2,192,128]{3,2,1,0:T(8,128)(2,1)} custom-call(s32[2]{0:T(128)S(1)} %pad_add_fusion.odd_ref, bf16[4,2,192,128]{3,2,1,0:T(8,128)(2,1)S(1)} %get-tuple-element.22.values_ref, bf16[4,2,192,128]{3,2,1,0:T(8,128)(2,1)S(1)} %get-tuple-element.23.act_ref, bf16[2,2,192,128]{3,2,1,0:T(8,128)(2,1)S(1)} %collective-permute-done.2.before_ref, ...), custom_call_target="tpu_custom_call" | custom-call | flops 2038431744 | bytes 1990656 | tf_op jit(solution)/shard_map/conv_layer_2/pallas_call | solution.py:116
  (10 shorter events, 0.2 us)
Async XLA Ops:
  0.0 1.0 %copy-start.1 = (bf16[4,2,192,128]{3,2,1,0:T(8,128)(2,1)S(1)}, bf16[4,2,192,128]{3,2,1,0:T(8,128)(2,1)}, u32[]{:S(2)}) copy-start(bf16[4,2,192,128]{3,2,1,0:T(8,128)(2,1)} %values_ref.3) | copy-start | bytes 1179652
  1.0 0.7 copy-start.3
  2.0 9.5 %collective-permute-start = (bf16[2,2,192,128]{3,2,0,1:T(8,128)(2,1)S(1)}, bf16[2,2,192,128]{3,2,0,1:T(8,128)(2,1)S(1)}, u32[]{:S(2)}, u32[]{:S(2)}) collective-permute-start(bf16[2,2,192,128]{3,2,0,1:T(8,128)(2,1)S(1)} %copy.17), channel_id=1, source_target_pairs={{0,4},{4,8},{8,12},{1,5},{5,9},{9,13},{2,6},{6,10},{10,14},{3,7},{... | collective-permute-start | bytes 589832 | tf_op jit(solution)/shard_map/ppermute | solution.py:145
  7.0 3.3 %copy-start = (bf16[3,27,192,192]{3,2,1,0:T(8,128)(2,1)S(1)}, bf16[3,27,192,192]{3,2,1,0:T(8,128)(2,1)}, u32[]{:S(2)}) copy-start(bf16[3,27,192,192]{3,2,1,0:T(8,128)(2,1)} %w_ref.1) | copy-start | bytes 17915908
  10.3 13.5 %copy-start.2 = (bf16[4,2,192,128]{3,2,1,0:T(8,128)(2,1)S(1)}, bf16[4,2,192,128]{3,2,1,0:T(8,128)(2,1)}, u32[]{:S(2)}) copy-start(bf16[4,2,192,128]{3,2,1,0:T(8,128)(2,1)} %values_ref.3) | copy-start | bytes 1179652
  10.3 13.5 %copy-start.4 = (f32[3,192]{1,0:T(4,128)S(1)}, f32[3,192]{1,0:T(4,128)}, u32[]{:S(2)}) copy-start(f32[3,192]{1,0:T(4,128)} %gains_ref.7) | copy-start | bytes 6916
  10.3 13.5 %copy-start.5 = (f32[3,192]{1,0:T(4,128)S(1)}, f32[3,192]{1,0:T(4,128)}, u32[]{:S(2)}) copy-start(f32[3,192]{1,0:T(4,128)} %biases_ref.5) | copy-start | bytes 6916
  27.3 8.4 %collective-permute-start.1 = (bf16[2,2,192,128]{3,2,1,0:T(8,128)(2,1)S(1)}, bf16[2,2,192,128]{3,2,1,0:T(8,128)(2,1)S(1)}, u32[]{:S(2)}, u32[]{:S(2)}) collective-permute-start(bf16[2,2,192,128]{3,2,1,0:T(8,128)(2,1)S(1)} %get-tuple-element.21), channel_id=1, source_target_pairs={{0,4},{4,8},{8,12},{1,5},{5,9},{9,13},{2,6},{6,10},{10,14},{3,7},{... | collective-permute-start | bytes 589832 | tf_op jit(solution)/shard_map/ppermute | solution.py:145
  51.0 8.8 %collective-permute-start.2 = (bf16[2,2,192,128]{3,2,1,0:T(8,128)(2,1)S(1)}, bf16[2,2,192,128]{3,2,1,0:T(8,128)(2,1)S(1)}, u32[]{:S(2)}, u32[]{:S(2)}) collective-permute-start(bf16[2,2,192,128]{3,2,1,0:T(8,128)(2,1)S(1)} %get-tuple-element.24), channel_id=1, source_target_pairs={{0,4},{4,8},{8,12},{1,5},{5,9},{9,13},{2,6},{6,10},{10,14},{3,7},{... | collective-permute-start | bytes 589832 | tf_op jit(solution)/shard_map/ppermute | solution.py:145

commit v3 on v1

v3 whole, which is shorter than its diff:
```python
import functools

import jax
import jax.numpy as jnp
from jax import lax
from jax.experimental import pallas as pl
from jax.experimental.pallas import tpu as pltpu
from jax.sharding import PartitionSpec as P

EPSILON = 1e-06
PAIR = 2
LANES = 128
VMEM = pl.BlockSpec(memory_space=pltpu.VMEM)
SMEM = pl.BlockSpec(memory_space=pltpu.SMEM)
LIMIT = 24 * 1024 * 1024


def rounded(lanes):
    return -(-lanes // LANES) * LANES


def column(row):
    return jnp.transpose(jnp.broadcast_to(row, (LANES, row.shape[1])))


def lane_of(lanes):
    return lax.broadcasted_iota(jnp.int32, (1, lanes), 1)


def filled(lanes, pitch):
    lane = lane_of(lanes)
    gaps = lane < 0
    for end in range(pitch - 1, lanes, pitch):
        gaps = gaps | (lane == end)
    return jnp.where(gaps, 0.0, 1.0)


def activated(values, gain, mask):
    squares = jnp.mean(values * values, axis=0, keepdims=True)
    normed = values * (lax.rsqrt(squares + EPSILON) * mask) * gain
    return (normed / (1.0 + jnp.exp(-normed))).astype(jnp.bfloat16)


def weights_kernel(place_ref, w_ref, out_ref):
    _, outs, ins = w_ref.shape
    flipped = place_ref[1]
    for time_tap in range(3):
        for row_tap in range(3):
            source = 9 * time_tap + 3 * (row_tap + flipped * (2 - 2 * row_tap))
            at = (3 * time_tap + row_tap) * ins
            out_ref[:, at : at + ins] = w_ref[pl.ds(source, 3)].reshape(3 * outs, ins)


def weights(place, conv_weight):
    layers, taps, outs, ins = conv_weight.shape
    return pl.pallas_call(
        weights_kernel,
        grid=(layers,),
        out_shape=jax.ShapeDtypeStruct((layers, 3 * outs, 9 * ins), conv_weight.dtype),
        in_specs=[SMEM, pl.BlockSpec((None, taps, outs, ins), lambda l: (l, 0, 0, 0))],
        out_specs=pl.BlockSpec((None, 3 * outs, 9 * ins), lambda l: (l, 0, 0)),
        compiler_params=pltpu.CompilerParams(vmem_limit_bytes=LIMIT),
        cost_estimate=pl.CostEstimate(flops=0, bytes_accessed=4 * conv_weight.size, transcendentals=0),
        name="weights",
    )(place, conv_weight)


def pack_kernel(halo, keep, place_ref, own_ref, mate_ref, far_ref, far_mate_ref, gains_ref, *out_refs):
    frames, rows, _, width = own_ref.shape
    core, group, outer = place_ref[0], place_ref[1], place_ref[2] == 1
    window = width // 2 + halo
    pitch = window + 1
    lanes = out_refs[0].shape[2]
    lane = lane_of(LANES)
    gain = column(gains_ref[0:1, :])
    mask = filled(lanes, pitch)
    first = core * (width - window)
    count = 2 * rows + halo
    for f in range(frames):
        blocks = [None] * (lanes // LANES)
        for row in range(count):
            near = row < 2 * rows
            local = row if near else 4 * rows - 1 - row
            at = local % rows
            side = group if near else 1 - group
            index = at + side * (rows - 1 - 2 * at)
            outermost = local < rows
            own, mate = (own_ref, mate_ref) if near else (far_mate_ref, far_ref)
            if not outermost:
                own, mate = mate, own
            line = jnp.where(outer, own[f, index], mate[f, index]).astype(jnp.float32)
            offset = row * pitch
            shift = lax.rem(offset % LANES + LANES - first, LANES)
            turned = pltpu.roll(line, shift, 1)
            low = offset % LANES
            block = offset // LANES
            here = (lane >= low) & (lane < low + window)
            piece = jnp.where(here, turned, 0.0)
            blocks[block] = piece if blocks[block] is None else blocks[block] + piece
            if low + window > LANES:
                piece = jnp.where(lane < low + window - LANES, turned, 0.0)
                blocks[block + 1] = piece
        for b, values in enumerate(blocks):
            part = slice(b * LANES, (b + 1) * LANES)
            out_refs[-1][f, :, part] = activated(values, gain, mask[:, part])
            if keep:
                out_refs[0][f, :, part] = values.astype(jnp.bfloat16)


def pack(halo, keep, place, own, mate, far, far_mate, gains):
    frames, rows, channels, width = own.shape
    lanes = rounded((2 * rows + halo) * (width // 2 + halo + 1))
    out = jax.ShapeDtypeStruct((frames, channels, lanes), jnp.bfloat16)
    return pl.pallas_call(
        functools.partial(pack_kernel, halo, keep),
        out_shape=(out,) * (1 + keep),
        in_specs=[SMEM] + [VMEM] * 5,
        out_specs=(VMEM,) * (1 + keep),
        compiler_params=pltpu.CompilerParams(vmem_limit_bytes=LIMIT),
        cost_estimate=pl.CostEstimate(
            flops=20 * frames * channels * lanes, bytes_accessed=8 * own.size, transcendentals=frames * channels * lanes
        ),
        name="pack",
    )(place, own, mate, far, far_mate, gains)


def conv_kernel(
    layer, last, pitch, half, place_ref, earlier_ref, act_ref, values_ref, w_ref, biases_ref, gains_ref, *refs
):
    outs, x_ref = refs[:-1], refs[-1]
    _, channels, lanes_in = act_ref.shape
    lanes = x_ref.shape[3] // PAIR
    first_row = lane_of(lanes_in) < pitch
    for j in range(2 * PAIR):
        ref = earlier_ref if j < PAIR else act_ref
        middle = ref[j % PAIR]
        wide = middle.astype(jnp.float32)
        above = jnp.where(first_row, 0.0, pltpu.roll(wide, pitch, 1)).astype(jnp.bfloat16)
        below = pltpu.roll(wide, lanes_in - pitch, 1).astype(jnp.bfloat16)
        for t in range(PAIR):
            if 0 <= j - t < 3:
                for tap, lines in enumerate((above, middle, below)):
                    x_ref[j - t, tap, :, t * lanes : (t + 1) * lanes] = lines[:, :lanes]
    sums = jnp.dot(
        w_ref[...], x_ref[...].reshape(9 * channels, PAIR * lanes), preferred_element_type=jnp.float32
    )
    bias = column(biases_ref[layer : layer + 1, :])
    start = lane_of(lanes) == 0
    if not last:
        gain = column(gains_ref[layer + 1 : layer + 2, :])
        mask = filled(lanes, pitch)
    for t in range(PAIR):
        part = sums[:, t * lanes : (t + 1) * lanes]
        conv = (
            jnp.where(start, 0.0, pltpu.roll(part[:channels], 1, 1))
            + part[channels : 2 * channels]
            + pltpu.roll(part[2 * channels :], lanes - 1, 1)
        )
        totals = []
        for b in range(lanes // LANES):
            at = slice(b * LANES, (b + 1) * LANES)
            total = (values_ref[t, :, at].astype(jnp.float32) + conv[:, at] + bias).astype(jnp.bfloat16)
            totals.append(total.astype(jnp.float32))
            if not last:
                outs[0][t, :, at] = total
                outs[1][t, :, at] = activated(totals[-1], gain, mask[:, at])
        if last:
            whole = jnp.concatenate(totals, axis=1)
            halo = pitch - 1 - half
            whole = jnp.where(place_ref[0] == 1, pltpu.roll(whole, lanes - halo, 1), whole)
            left = lane_of(LANES) < half

            def rows_of(row):
                one = whole if row == 0 else pltpu.roll(whole, lanes - row * pitch, 1)
                two = pltpu.roll(whole, lanes - (row + 1) * pitch + half, 1)
                return jnp.where(left, one[:, :LANES], two[:, :LANES])

            outermost, inner = rows_of(0), rows_of(2)
            outer = place_ref[2] == 1
            outs[0][t] = jnp.where(outer, outermost, inner).astype(jnp.bfloat16)
            outs[1][t] = jnp.where(outer, inner, outermost).astype(jnp.bfloat16)


def conv(layer, last, pitch, rows_left, half, place, earlier, act, values, weight, biases, gains):
    _, channels, _ = act.shape
    lanes = rounded(rows_left * pitch)
    out = jax.ShapeDtypeStruct((PAIR, channels, LANES if last else lanes), jnp.bfloat16)
    weight_spec = pl.BlockSpec((None,) + weight.shape[1:], lambda i: (layer, 0, 0))
    return pl.pallas_call(
        functools.partial(conv_kernel, layer, last, pitch, half),
        grid=(1,),
        out_shape=(out, out),
        in_specs=[SMEM] + [VMEM] * 3 + [weight_spec] + [VMEM] * 2,
        out_specs=(VMEM, VMEM),
        scratch_shapes=[pltpu.VMEM((3, 3, channels, PAIR * lanes), jnp.bfloat16)],
        compiler_params=pltpu.CompilerParams(vmem_limit_bytes=LIMIT),
        cost_estimate=pl.CostEstimate(
            flops=54 * channels * channels * PAIR * lanes,
            bytes_accessed=2 * weight.size // weight.shape[0],
            transcendentals=PAIR * channels * lanes,
        ),
        name=f"conv_{layer}",
    )(place, earlier, act, values, weight, biases, gains)


def join_kernel(place_ref, *refs):
    out_ref = refs[-1]
    kept, got = refs[: len(refs) // 2], refs[len(refs) // 2 : -1]
    _, rows, _, width = out_ref.shape
    half = width // 2
    first, group = place_ref[0] == 0, place_ref[1]
    left_half = lane_of(width) < half
    for p in range(len(kept)):
        for t in range(PAIR):
            mine, theirs = kept[p][t].astype(jnp.float32), got[p][t].astype(jnp.float32)
            left, right = jnp.where(first, mine, theirs), jnp.where(first, theirs, mine)
            lines = (
                jnp.where(left_half, left, pltpu.roll(right, half, 1)),
                jnp.where(left_half, pltpu.roll(left, half, 1), right),
            )
            for j in range(rows):
                out_ref[PAIR * p + t, j + group * (rows - 1 - 2 * j)] = lines[j].astype(jnp.bfloat16)


def join(place, kept, got, shape):
    return pl.pallas_call(
        join_kernel,
        out_shape=jax.ShapeDtypeStruct(shape, jnp.bfloat16),
        in_specs=[SMEM] + [VMEM] * (2 * len(kept)),
        out_specs=VMEM,
        compiler_params=pltpu.CompilerParams(vmem_limit_bytes=LIMIT),
        name="join",
    )(place, *kept, *got)


def on_device(latents, conv_weight, norm_gains, biases):
    layers = conv_weight.shape[0]
    frames, rows, channels, width = latents.shape
    strips, blocks = lax.axis_size("rows"), lax.axis_size("tm")
    assert strips == 4 and rows == 2 and frames % PAIR == 0 and width == LANES
    strip = lax.axis_index("rows").astype(jnp.int32)
    core, group = strip & 1, strip >> 1
    place = jnp.stack([core, group, (core == group).astype(jnp.int32)])

    def mate_of(block):
        return lax.ppermute(block, "rows", [(i, i ^ 1) for i in range(strips)])

    def earlier_of(block):
        return lax.ppermute(block, "tm", [(i, i + 1) for i in range(blocks - 1)])

    tail = latents[frames - PAIR :]
    far = lax.ppermute(latents, "rows", [(i, i ^ 2) for i in range(strips)])
    mate = mate_of(latents)
    before = earlier_of(tail)
    across = [
        (z * strips + r, (z + 1) * strips + (r ^ 2)) for z in range(blocks - 1) for r in range(strips)
    ]
    far_before = lax.ppermute(tail, ("tm", "rows"), across)
    weight = weights(place, conv_weight)
    far_mate = mate_of(far)
    both = jnp.concatenate([before, far_before], axis=0)
    both_mate = mate_of(both)

    values, act = pack(layers, True, place, latents, mate, far, far_mate, norm_gains)
    halo = pack(layers, False, place, before, both_mate[:PAIR], far_before, both_mate[PAIR:], norm_gains)[0]
    pitch = width // 2 + layers + 1
    pairs = frames // PAIR
    values = [values[PAIR * p : PAIR * (p + 1)] for p in range(pairs)]
    act = [act[PAIR * p : PAIR * (p + 1)] for p in range(pairs)]
    for layer in range(layers):
        last = layer == layers - 1
        rows_left = 2 * rows + layers - 1 - layer
        results = [None] * pairs
        next_halo = None
        for p in reversed(range(pairs)):
            earlier = act[p - 1] if p else halo
            results[p] = conv(
                layer, last, pitch, rows_left, width // 2, place, earlier, act[p], values[p], weight, biases, norm_gains
            )
            if p == pairs - 1 and not last:
                next_halo = earlier_of(results[p][1])
        values, act = [r[0] for r in results], [r[1] for r in results]
        halo = next_halo
    got = [mate_of(send) for send in act]
    return join(place, values, got, latents.shape)


def solution(mesh):
    in_specs = (P(("clips", "tm"), "rows", None, None), P(), P(), P())
    out_specs = P(("clips", "tm"), "rows", None, None)
    return jax.shard_map(on_device, mesh=mesh, in_specs=in_specs, out_specs=out_specs, check_vma=False)
```

time: 60 us -> 60.3 us (level)
  the two profiles are of different devices: /device:TPU:25 before, /device:TPU:0 now
where the time goes in v3:
time: 60.3 us; the launch traced here: 60.1 us
  Pallas kernels  24.4 us (40%)
  starting transfers between devices  19.3 us (32%)
  waiting for transfers between devices  11.7 us (19%)
  local copies, waits for them, and re-layouts  4.35 us (7%)
    pallas_call x6, Pallas kernels, conv(): pl.pallas_call(functools.partial(conv_kernel, layer, last, pitch, half),...  18.3 us
    ppermute x3, starting transfers between devices, earlier_of(): return lax.ppermute(block, 'tm', [(i, i + 1) for i in range(blocks - 1)])  11.6 us
    ppermute x1, waiting for transfers between devices, on_device(): far = lax.ppermute(latents, 'rows', [(i, i ^ 2) for i in range(strips)])  9.39 us
    ppermute x1, starting transfers between devices, on_device(): far_before = lax.ppermute(tail, ('tm', 'rows'), across)  4.6 us
    unnamed x8, local copies, waits for them, and re-layouts  3.27 us
    pallas_call x2, Pallas kernels, pack(): pl.pallas_call(functools.partial(pack_kernel, halo, keep), out_shape=(out...  2.99 us
    ppermute x1, starting transfers between devices, on_device(): far = lax.ppermute(latents, 'rows', [(i, i ^ 2) for i in range(strips)])  2.94 us
    pallas_call x1, Pallas kernels, weights(): pl.pallas_call(weights_kernel, grid=(layers,), out_shape=jax.ShapeDtypeSt...  1.69 us
  transfers between devices with their start and end apart: 10, of which 4 were waited for; matrix products, arithmetic and copies ran while one was open for 2% of the time, Pallas kernels for 38%

profile of v3, /device:TPU:0, one launch (start us, length us, event | category | flops | bytes accessed | tf_op | source)
XLA Modules:
  0.0 60.1 jit_solution(5502959009799009903)
XLA Ops:
  0.0 2.9 %collective-permute-start.4 = (bf16[4,2,192,128]{3,2,1,0:T(8,128)(2,1)}, bf16[4,2,192,128]{3,2,1,0:T(8,128)(2,1)S(1)}, u32[]{:S(2)}, u32[]{:S(2)}) collective-permute-start(bf16[4,2,192,128]{3,2,1,0:T(8,128)(2,1)} %own_ref.1), channel_id=1, source_target_pairs={{0,2},{1,3},{2,0},{3,1},{4,6},{5,7},{6,4},{7,5},{8,10},{9,11},{10,... | collective-permute-start | bytes 1179656 | tf_op jit(solution)/shard_map/ppermute | solution.py:252
  2.9 0.0 collective-permute-start.3
  2.9 9.4 %collective-permute-done.4.far_ref = bf16[4,2,192,128]{3,2,1,0:T(8,128)(2,1)S(1)} collective-permute-done((bf16[4,2,192,128]{3,2,1,0:T(8,128)(2,1)}, bf16[4,2,192,128]{3,2,1,0:T(8,128)(2,1)S(1)}, u32[]{:S(2)}, u32[]{:S(2)}) %collective-permute-start.4) | collective-permute-done | bytes 393248 | tf_op jit(solution)/shard_map/ppermute | solution.py:252
  12.3 0.0 collective-permute-start.5
  12.3 0.9 %slice.21 = bf16[2,2,192,128]{3,2,1,0:T(8,128)(2,1)S(1)} slice(bf16[4,2,192,128]{3,2,1,0:T(8,128)(2,1)} %own_ref.1), slice={[2:4], [0:2], [0:192], [0:128]} | slice | bytes 393216 | tf_op jit(solution)/shard_map/slice | solution.py:251
  13.3 4.6 %collective-permute-start.1 = (bf16[2,2,192,128]{3,2,1,0:T(8,128)(2,1)S(1)}, bf16[2,2,192,128]{3,2,1,0:T(8,128)(2,1)S(1)}, u32[]{:S(2)}, u32[]{:S(2)}) collective-permute-start(bf16[2,2,192,128]{3,2,1,0:T(8,128)(2,1)S(1)} %slice.21), channel_id=1, source_target_pairs={{0,6},{1,7},{2,4},{3,5},{4,10},{5,11},{6,8},{7,9},{8,14},{9,15},{1... | collective-permute-start | bytes 589832 | tf_op jit(solution)/shard_map/ppermute | solution.py:258
  17.9 3.5 %collective-permute-start = (bf16[2,2,192,128]{3,2,1,0:T(8,128)(2,1)S(1)}, bf16[2,2,192,128]{3,2,1,0:T(8,128)(2,1)S(1)}, u32[]{:S(2)}, u32[]{:S(2)}) collective-permute-start(bf16[2,2,192,128]{3,2,1,0:T(8,128)(2,1)S(1)} %slice.21), channel_id=1, source_target_pairs={{0,4},{4,8},{8,12},{1,5},{5,9},{9,13},{2,6},{6,10},{10,14},{3,7},{... | collective-permute-start | bytes 589832 | tf_op jit(solution)/shard_map/ppermute | solution.py:249
  21.4 0.1 pad_add_fusion.place_ref
  21.5 3.3 %copy-done = bf16[3,27,192,192]{3,2,1,0:T(8,128)(2,1)S(1)} copy-done((bf16[3,27,192,192]{3,2,1,0:T(8,128)(2,1)S(1)}, bf16[3,27,192,192]{3,2,1,0:T(8,128)(2,1)}, u32[]{:S(2)}) %copy-start) | copy-done | bytes 5971992
  24.7 1.7 %weights.1.w_ref = bf16[3,576,1728]{2,1,0:T(8,128)(2,1)S(1)} custom-call(s32[3]{0:T(128)S(1)} %pad_add_fusion.place_ref, bf16[3,27,192,192]{3,2,1,0:T(8,128)(2,1)S(1)} %copy-done), custom_call_target="tpu_custom_call" | custom-call | bytes 11943936 | tf_op jit(solution)/shard_map/weights/pallas_call | solution.py:56
  26.4 0.5 collective-permute-done.own_ref
  26.9 0.1 collective-permute-start.2
  27.0 0.0 collective-permute-done.3.mate_ref
  27.1 1.8 %pack.3 = (bf16[4,192,512]{2,1,0:T(8,128)(2,1)S(1)}, bf16[4,192,512]{2,1,0:T(8,128)(2,1)S(1)}) custom-call(s32[3]{0:T(128)S(1)} %pad_add_fusion.place_ref, bf16[4,2,192,128]{3,2,1,0:T(8,128)(2,1)S(1)} %copy-done.1, bf16[4,2,192,128]{3,2,1,0:T(8,128)(2,1)S(1)} %collective-permute-done.3.mate_ref, bf16[4,2,192,128]{3,2,1,0:T(8,128)(2,1)S(1)} %collective-permute-done.4.far_ref, ...), custom_call_target="tpu_custom_call" | custom-call | flops 7864320 | bytes 1572864 | tf_op jit(solution)/shard_map/pack/pallas_call | solution.py:114
  28.9 0.1 fusion
  29.0 3.3 %conv_0.3 = (bf16[2,192,512]{2,1,0:T(8,128)(2,1)S(1)}, bf16[2,192,512]{2,1,0:T(8,128)(2,1)S(1)}) custom-call(s32[3]{0:T(128)S(1)} %pad_add_fusion.place_ref, bf16[2,192,512]{2,1,0:T(8,128)(2,1)S(1)} %get-tuple-element.39.act_ref.earlier_ref, bf16[2,192,512]{2,1,0:T(8,128)(2,1)S(1)} %get-tuple-element.40.act_ref, ...), custom_call_target="tpu_custom_call" | custom-call | flops 2038431744 | bytes 1990656 | tf_op jit(solution)/shard_map/conv_0/pallas_call | solution.py:189
  32.3 4.4 %collective-permute-start.7 = (bf16[2,192,512]{2,1,0:T(8,128)(2,1)S(1)}, bf16[2,192,512]{2,1,0:T(8,128)(2,1)S(1)}, u32[]{:S(2)}, u32[]{:S(2)}) collective-permute-start(bf16[2,192,512]{2,1,0:T(8,128)(2,1)S(1)} %get-tuple-element.22.act_ref), channel_id=1, source_target_pairs={{0,4},{4,8},{8,12},{1,5},{5,9},{9,13},{2,6},{6,10},{10,14},{3,7},{... | collective-permute-start | bytes 1179656 | tf_op jit(solution)/shard_map/ppermute | solution.py:249
  36.7 0.0 collective-permute-done.2
  36.8 1.2 %pack.2.earlier_ref = bf16[2,192,512]{2,1,0:T(8,128)(2,1)S(1)} custom-call(s32[3]{0:T(128)S(1)} %pad_add_fusion.place_ref, bf16[2,2,192,128]{3,2,1,0:T(8,128)(2,1)S(1)} %collective-permute-done.own_ref, bf16[2,2,192,128]{3,2,1,0:T(8,128)(2,1)S(1)} %get-tuple-element.38.mate_ref, bf16[2,2,192,128]{3,2,1,0:T(8,128)(2,1)S(1)} %collective-permute-done.1.far_ref, ...), custom_call_target="tpu_custom_call" | custom-call | flops 3932160 | bytes 786432 | tf_op jit(solution)/shard_map/pack/pallas_call | solution.py:114
  38.0 3.3 %conv_0.2 = (bf16[2,192,512]{2,1,0:T(8,128)(2,1)S(1)}, bf16[2,192,512]{2,1,0:T(8,128)(2,1)S(1)}) custom-call(s32[3]{0:T(128)S(1)} %pad_add_fusion.place_ref, bf16[2,192,512]{2,1,0:T(8,128)(2,1)S(1)} %pack.2.earlier_ref, bf16[2,192,512]{2,1,0:T(8,128)(2,1)S(1)} %get-tuple-element.39.act_ref.earlier_ref, ...), custom_call_target="tpu_custom_call" | custom-call | flops 2038431744 | bytes 1990656 | tf_op jit(solution)/shard_map/conv_0/pallas_call | solution.py:189
  41.4 2.9 %conv_1.2 = (bf16[2,192,384]{2,1,0:T(8,128)(2,1)S(1)}, bf16[2,192,384]{2,1,0:T(8,128)(2,1)S(1)}) custom-call(s32[3]{0:T(128)S(1)} %pad_add_fusion.place_ref, bf16[2,192,512]{2,1,0:T(8,128)(2,1)S(1)} %get-tuple-element.21.earlier_ref.act_ref, bf16[2,192,512]{2,1,0:T(8,128)(2,1)S(1)} %get-tuple-element.22.act_ref, ...), custom_call_target="tpu_custom_call" | custom-call | flops 1528823808 | bytes 1990656 | tf_op jit(solution)/shard_map/conv_1/pallas_call | solution.py:189
  44.3 3.7 %collective-permute-start.6 = (bf16[2,192,384]{2,1,0:T(8,128)(2,1)S(1)}, bf16[2,192,384]{2,1,0:T(8,128)(2,1)S(1)}, u32[]{:S(2)}, u32[]{:S(2)}) collective-permute-start(bf16[2,192,384]{2,1,0:T(8,128)(2,1)S(1)} %get-tuple-element.24.act_ref), channel_id=1, source_target_pairs={{0,4},{4,8},{8,12},{1,5},{5,9},{9,13},{2,6},{6,10},{10,14},{3,7},{... | collective-permute-start | bytes 884744 | tf_op jit(solution)/shard_map/ppermute | solution.py:249
  47.9 0.0 collective-permute-done.7.earlier_ref
  48.0 2.9 %conv_1.3 = (bf16[2,192,384]{2,1,0:T(8,128)(2,1)S(1)}, bf16[2,192,384]{2,1,0:T(8,128)(2,1)S(1)}) custom-call(s32[3]{0:T(128)S(1)} %pad_add_fusion.place_ref, bf16[2,192,512]{2,1,0:T(8,128)(2,1)S(1)} %collective-permute-done.7.earlier_ref, bf16[2,192,512]{2,1,0:T(8,128)(2,1)S(1)} %get-tuple-element.21.earlier_ref.act_ref, ...), custom_call_target="tpu_custom_call" | custom-call | flops 1528823808 | bytes 1990656 | tf_op jit(solution)/shard_map/conv_1/pallas_call | solution.py:189
  50.9 2.9 %conv_2.3 = (bf16[2,192,128]{2,1,0:T(8,128)(2,1)S(1)}, bf16[2,192,128]{2,1,0:T(8,128)(2,1)S(1)}) custom-call(s32[3]{0:T(128)S(1)} %pad_add_fusion.place_ref, bf16[2,192,384]{2,1,0:T(8,128)(2,1)S(1)} %get-tuple-element.26.act_ref.earlier_ref, bf16[2,192,384]{2,1,0:T(8,128)(2,1)S(1)} %get-tuple-element.24.act_ref, ...), custom_call_target="tpu_custom_call" | custom-call | flops 1528823808 | bytes 1990656 | tf_op jit(solution)/shard_map/conv_2/pallas_call | solution.py:189
  53.7 0.1 collective-permute-start.9
  53.8 0.5 collective-permute-done.6.earlier_ref
  54.3 2.9 %conv_2.2 = (bf16[2,192,128]{2,1,0:T(8,128)(2,1)S(1)}, bf16[2,192,128]{2,1,0:T(8,128)(2,1)S(1)}) custom-call(s32[3]{0:T(128)S(1)} %pad_add_fusion.place_ref, bf16[2,192,384]{2,1,0:T(8,128)(2,1)S(1)} %collective-permute-done.6.earlier_ref, bf16[2,192,384]{2,1,0:T(8,128)(2,1)S(1)} %get-tuple-element.26.act_ref.earlier_ref, ...), custom_call_target="tpu_custom_call" | custom-call | flops 1528823808 | bytes 1990656 | tf_op jit(solution)/shard_map/conv_2/pallas_call | solution.py:189
  57.2 0.1 collective-permute-start.8
  57.3 0.0 collective-permute-done.9.refs_3_
  57.3 1.3 %collective-permute-done.8.refs_2_ = bf16[2,192,128]{2,1,0:T(8,128)(2,1)S(1)} collective-permute-done((bf16[2,192,128]{2,1,0:T(8,128)(2,1)S(1)}, bf16[2,192,128]{2,1,0:T(8,128)(2,1)S(1)}, u32[]{:S(2)}, u32[]{:S(2)}) %collective-permute-start.8) | collective-permute-done | bytes 98336 | tf_op jit(solution)/shard_map/ppermute | solution.py:246
  58.6 1.5 %join.1 = bf16[4,2,192,128]{3,2,1,0:T(8,128)(2,1)} custom-call(s32[3]{0:T(128)S(1)} %pad_add_fusion.place_ref, bf16[2,192,128]{2,1,0:T(8,128)(2,1)S(1)} %get-tuple-element.28.refs_0_, bf16[2,192,128]{2,1,0:T(8,128)(2,1)S(1)} %get-tuple-element.30.refs_1_, bf16[2,192,128]{2,1,0:T(8,128)(2,1)S(1)} %collective-permute-done.8.refs_2_, ...), custom_call_target="tpu_custom_call" | custom-call | tf_op jit(solution)/shard_map/join/pallas_call | solution.py:226
  (11 shorter events, 0.1 us)
Async XLA Ops:
  0.0 27.0 %copy-start.1 = (bf16[4,2,192,128]{3,2,1,0:T(8,128)(2,1)S(1)}, bf16[4,2,192,128]{3,2,1,0:T(8,128)(2,1)}, u32[]{:S(2)}) copy-start(bf16[4,2,192,128]{3,2,1,0:T(8,128)(2,1)} %own_ref.1) | copy-start | bytes 1179652
  0.0 27.1 %copy-start.2 = (f32[3,192]{1,0:T(4,128)S(1)}, f32[3,192]{1,0:T(4,128)}, u32[]{:S(2)}) copy-start(f32[3,192]{1,0:T(4,128)} %gains_ref.15) | copy-start | bytes 6916
  0.0 12.3 %collective-permute-start.4 = (bf16[4,2,192,128]{3,2,1,0:T(8,128)(2,1)}, bf16[4,2,192,128]{3,2,1,0:T(8,128)(2,1)S(1)}, u32[]{:S(2)}, u32[]{:S(2)}) collective-permute-start(bf16[4,2,192,128]{3,2,1,0:T(8,128)(2,1)} %own_ref.1), channel_id=1, source_target_pairs={{0,2},{1,3},{2,0},{3,1},{4,6},{5,7},{6,4},{7,5},{8,10},{9,11},{10,... | collective-permute-start | bytes 1179656 | tf_op jit(solution)/shard_map/ppermute | solution.py:252
  2.9 24.1 %collective-permute-start.3 = (bf16[4,2,192,128]{3,2,1,0:T(8,128)(2,1)}, bf16[4,2,192,128]{3,2,1,0:T(8,128)(2,1)S(1)}, u32[]{:S(2)}, u32[]{:S(2)}) collective-permute-start(bf16[4,2,192,128]{3,2,1,0:T(8,128)(2,1)} %own_ref.1), channel_id=1, source_target_pairs={{0,1},{1,0},{2,3},{3,2},{4,5},{5,4},{6,7},{7,6},{8,9},{9,8},{10,11... | collective-permute-start | bytes 1179656 | tf_op jit(solution)/shard_map/ppermute | solution.py:246
  12.3 14.7 %collective-permute-start.5 = (bf16[4,2,192,128]{3,2,1,0:T(8,128)(2,1)S(1)}, bf16[4,2,192,128]{3,2,1,0:T(8,128)(2,1)S(1)}, u32[]{:S(2)}, u32[]{:S(2)}) collective-permute-start(bf16[4,2,192,128]{3,2,1,0:T(8,128)(2,1)S(1)} %collective-permute-done.4.far_ref), channel_id=1, source_target_pairs={{0,1},{1,0},{2,3},{3,2},{4,5},{5,4},{6,7},{7,6},{8,9},{9,8},{10,11... | collective-permute-start | bytes 1179656 | tf_op jit(solution)/shard_map/ppermute | solution.py:246
  13.3 13.2 %collective-permute-start.1 = (bf16[2,2,192,128]{3,2,1,0:T(8,128)(2,1)S(1)}, bf16[2,2,192,128]{3,2,1,0:T(8,128)(2,1)S(1)}, u32[]{:S(2)}, u32[]{:S(2)}) collective-permute-start(bf16[2,2,192,128]{3,2,1,0:T(8,128)(2,1)S(1)} %slice.21), channel_id=1, source_target_pairs={{0,6},{1,7},{2,4},{3,5},{4,10},{5,11},{6,8},{7,9},{8,14},{9,15},{1... | collective-permute-start | bytes 589832 | tf_op jit(solution)/shard_map/ppermute | solution.py:258
  17.9 9.0 %collective-permute-start = (bf16[2,2,192,128]{3,2,1,0:T(8,128)(2,1)S(1)}, bf16[2,2,192,128]{3,2,1,0:T(8,128)(2,1)S(1)}, u32[]{:S(2)}, u32[]{:S(2)}) collective-permute-start(bf16[2,2,192,128]{3,2,1,0:T(8,128)(2,1)S(1)} %slice.21), channel_id=1, source_target_pairs={{0,4},{4,8},{8,12},{1,5},{5,9},{9,13},{2,6},{6,10},{10,14},{3,7},{... | collective-permute-start | bytes 589832 | tf_op jit(solution)/shard_map/ppermute | solution.py:249
  21.5 3.3 %copy-start = (bf16[3,27,192,192]{3,2,1,0:T(8,128)(2,1)S(1)}, bf16[3,27,192,192]{3,2,1,0:T(8,128)(2,1)}, u32[]{:S(2)}) copy-start(bf16[3,27,192,192]{3,2,1,0:T(8,128)(2,1)} %w_ref.1) | copy-start | bytes 17915908
  24.7 4.2 %copy-start.3 = (f32[3,192]{1,0:T(4,128)S(1)}, f32[3,192]{1,0:T(4,128)}, u32[]{:S(2)}) copy-start(f32[3,192]{1,0:T(4,128)} %biases_ref.11) | copy-start | bytes 6916
  26.9 9.8 %collective-permute-start.2 = (bf16[4,2,192,128]{3,2,1,0:T(8,128)(2,1)S(1)}, bf16[4,2,192,128]{3,2,1,0:T(8,128)(2,1)S(1)}, u32[]{:S(2)}, u32[]{:S(2)}) collective-permute-start(bf16[4,2,192,128]{3,2,1,0:T(8,128)(2,1)S(1)} %pad_maximum_fusion), channel_id=1, source_target_pairs={{0,1},{1,0},{2,3},{3,2},{4,5},{5,4},{6,7},{7,6},{8,9},{9,8},{10,11... | collective-permute-start | bytes 1179656 | tf_op jit(solution)/shard_map/ppermute | solution.py:246
  32.3 15.6 %collective-permute-start.7 = (bf16[2,192,512]{2,1,0:T(8,128)(2,1)S(1)}, bf16[2,192,512]{2,1,0:T(8,128)(2,1)S(1)}, u32[]{:S(2)}, u32[]{:S(2)}) collective-permute-start(bf16[2,192,512]{2,1,0:T(8,128)(2,1)S(1)} %get-tuple-element.22.act_ref), channel_id=1, source_target_pairs={{0,4},{4,8},{8,12},{1,5},{5,9},{9,13},{2,6},{6,10},{10,14},{3,7},{... | collective-permute-start | bytes 1179656 | tf_op jit(solution)/shard_map/ppermute | solution.py:249
  44.3 10.1 %collective-permute-start.6 = (bf16[2,192,384]{2,1,0:T(8,128)(2,1)S(1)}, bf16[2,192,384]{2,1,0:T(8,128)(2,1)S(1)}, u32[]{:S(2)}, u32[]{:S(2)}) collective-permute-start(bf16[2,192,384]{2,1,0:T(8,128)(2,1)S(1)} %get-tuple-element.24.act_ref), channel_id=1, source_target_pairs={{0,4},{4,8},{8,12},{1,5},{5,9},{9,13},{2,6},{6,10},{10,14},{3,7},{... | collective-permute-start | bytes 884744 | tf_op jit(solution)/shard_map/ppermute | solution.py:249
  53.7 3.6 %collective-permute-start.9 = (bf16[2,192,128]{2,1,0:T(8,128)(2,1)S(1)}, bf16[2,192,128]{2,1,0:T(8,128)(2,1)S(1)}, u32[]{:S(2)}, u32[]{:S(2)}) collective-permute-start(bf16[2,192,128]{2,1,0:T(8,128)(2,1)S(1)} %get-tuple-element.32), channel_id=1, source_target_pairs={{0,1},{1,0},{2,3},{3,2},{4,5},{5,4},{6,7},{7,6},{8,9},{9,8},{10,11... | collective-permute-start | bytes 294920 | tf_op jit(solution)/shard_map/ppermute | solution.py:246
  57.2 1.4 %collective-permute-start.8 = (bf16[2,192,128]{2,1,0:T(8,128)(2,1)S(1)}, bf16[2,192,128]{2,1,0:T(8,128)(2,1)S(1)}, u32[]{:S(2)}, u32[]{:S(2)}) collective-permute-start(bf16[2,192,128]{2,1,0:T(8,128)(2,1)S(1)} %get-tuple-element.31), channel_id=1, source_target_pairs={{0,1},{1,0},{2,3},{3,2},{4,5},{5,4},{6,7},{7,6},{8,9},{9,8},{10,11... | collective-permute-start | bytes 294920 | tf_op jit(solution)/shard_map/ppermute | solution.py:246
